TPU v7x, 256 devices: a whole 4x4x8 slice. The times are simulated.
256 devices in a mesh: step: 16 (over y, x), cfg: 2 (over core), seq: 8 (over z).
Axes of the slice: x: 4, y: 4, z: 8, core: 2. Of those that a mesh axis runs over, the one named last changes fastest.
Arguments:
- initial_noisy_clip: float32 [2048, 1024], P('seq'), may hold values from -6 to 6
- sampler_noise_level_ordinal: int32 [16], P('step'), may hold values from 0 to 49
- classifier_free_strength: float32 [16], P('step'), may hold values from 1.5 to 4
- integrator_increment: float32 [16], P('step'), may hold values from 0.03 to 0.12
- noise_level_affine_gates: bfloat16 [50, 3072], replicated, may hold values from -3 to 3
- guided_affine_gate_pairs: bfloat16 [2, 3072], P('cfg'), may hold values from -3 to 3
- attention_input_projectors: bfloat16 [1024, 3072], replicated, may hold values from -0.1875 to 0.1875
- attention_merge_projector: bfloat16 [1024, 1024], replicated, may hold values from -0.1875 to 0.1875
- attention_sharpness: float32 [16], replicated, may hold values from 1 to 4
Outputs:
- trajectory: float32 [16, 2048, 1024], P('step', 'seq')
All inputs are finite; a program needn't handle non-finite values.
Results may differ from a plain program's by a relative error of at most 0.0045.
Values may be sent and summed in bfloat16 or wider, within the bound.
A program may use at most 128 MiB of HBM per device.

v0:
```python
import math

import jax
import jax.numpy as jnp
from jax import lax
from jax.sharding import PartitionSpec as P

ATTENTION_GROUPS = 16
SWEEPS = 2


def entering(value, axis, join, neutral):
    count, mine = (lax.axis_size(axis), lax.axis_index(axis))
    pieces = lax.all_gather(value, axis)
    total = jnp.full_like(value, 0) + jnp.asarray(neutral, value.dtype)

    def turn(position, total):
        longer = join(total, pieces[position])
        return jnp.where(position < mine, longer, total)

    return lax.fori_loop(0, count - 1, turn, total)


def partner_2(block, axis, bit):
    count = lax.axis_size(axis)
    route = []
    for low in range(count):
        high = low | 1 << bit
        if high != low and high < count:
            route += [(low, high), (high, low)]
    return lax.ppermute(block, axis, route)


def normalize_rows(values):
    return values * lax.rsqrt(jnp.mean(values * values, axis=-1, keepdims=True) + 1e-06)


def attend_pairs(block):
    frames = block.shape[0]
    pair_count = block.shape[2] * block.shape[3]
    subspace_dimension = block.shape[4] // 2
    separated = block.reshape(frames, 3, pair_count * 2, subspace_dimension)
    probe_vectors_stacked = separated[:, 0]
    key_rows = separated[:, 1]
    value_rows = separated[:, 2]
    block_rows = min(512, frames)
    block_count = frames // block_rows

    def block_attention(query_block):
        scores = jnp.einsum(
            "qhd,khd->hqk", query_block, key_rows, preferred_element_type=jnp.float32
        )
        row_max = jnp.max(scores, axis=-1, keepdims=True)
        powers = jnp.exp(scores - row_max)
        weights = (powers / jnp.sum(powers, axis=-1, keepdims=True)).astype(jnp.bfloat16)
        return jnp.einsum(
            "hqk,khd->qhd", weights, value_rows, preferred_element_type=jnp.float32
        ).astype(jnp.bfloat16)

    result = lax.map(
        block_attention,
        probe_vectors_stacked.reshape(block_count, block_rows, pair_count * 2, subspace_dimension),
    )
    return result.reshape(frames, 1, pair_count, 2 * subspace_dimension)


def add_terms(earlier, later):
    return earlier + later


def local(
    initial_noisy_clip,
    sampler_noise_level_ordinal,
    classifier_free_strength,
    integrator_increment,
    noise_level_affine_gates,
    guided_affine_gate_pairs,
    attention_input_projectors,
    attention_merge_projector,
    attention_sharpness,
):
    frame_rows = initial_noisy_clip.shape[0]
    width = initial_noisy_clip.shape[1]
    subspace_dimension = width // ATTENTION_GROUPS
    seq_count = lax.axis_size("seq")
    pairs_each = ATTENTION_GROUPS // (2 * seq_count)
    table_rows = noise_level_affine_gates.shape[0]
    chosen = (jnp.arange(table_rows, dtype=jnp.int32) == sampler_noise_level_ordinal[0]).astype(
        jnp.bfloat16
    )[None]
    affine_gate_entries = jnp.dot(
        chosen, noise_level_affine_gates, preferred_element_type=jnp.float32
    )[0] + guided_affine_gate_pairs[0].astype(jnp.float32)
    shift = affine_gate_entries[:width]
    scale_part = affine_gate_entries[width : 2 * width]
    gate = affine_gate_entries[2 * width :]
    scale_now = classifier_free_strength[0]
    step_now = integrator_increment[0]
    branch_slot = lax.axis_index("cfg")
    reciprocal_root_dimension = attention_sharpness[:, None] / math.sqrt(subspace_dimension)
    noisy_pose_sequence = initial_noisy_clip
    for sweep_index in range(SWEEPS):
        average = jnp.mean(noisy_pose_sequence, axis=-1, keepdims=True)
        centred = noisy_pose_sequence - average
        variance = jnp.mean(centred * centred, axis=-1, keepdims=True)
        normed = centred * lax.rsqrt(variance + 1e-06)
        hidden = (normed * (1.0 + scale_part) + shift).astype(jnp.bfloat16)
        qkv = jnp.dot(
            hidden, attention_input_projectors, preferred_element_type=jnp.float32
        ).reshape(frame_rows, 3, ATTENTION_GROUPS, subspace_dimension)
        probe_vectors_stacked = (normalize_rows(qkv[:, 0]) * reciprocal_root_dimension).astype(
            jnp.bfloat16
        )
        key_rows = normalize_rows(qkv[:, 1]).astype(jnp.bfloat16)
        value_rows = qkv[:, 2].astype(jnp.bfloat16)
        packed = jnp.stack([probe_vectors_stacked, key_rows, value_rows], axis=1).reshape(
            frame_rows, 3, seq_count, pairs_each, 2 * subspace_dimension
        )
        attended = attend_pairs(
            lax.all_to_all(packed, "seq", split_axis=2, concat_axis=0, tiled=True)
        )
        attended = lax.all_to_all(attended, "seq", split_axis=0, concat_axis=1, tiled=True).reshape(
            frame_rows, width
        )
        projected = jnp.dot(attended, attention_merge_projector, preferred_element_type=jnp.float32)
        branch = (gate * projected).astype(jnp.bfloat16)
        partner = partner_2(branch, "cfg", 0)
        cond_branch = jnp.where(branch_slot == 0, branch, partner).astype(jnp.float32)
        uncond_branch = jnp.where(branch_slot == 0, partner, branch).astype(jnp.float32)
        sweep_drift = step_now * (
            noisy_pose_sequence + scale_now * cond_branch + (1.0 - scale_now) * uncond_branch
        )
        lower = entering(sweep_drift, "step", add_terms, jnp.zeros_like(sweep_drift))
        noisy_pose_sequence = initial_noisy_clip + (
            lower + sweep_drift if sweep_index == SWEEPS - 1 else lower
        )
    return noisy_pose_sequence[None]


def solution(mesh):
    placed = (P("seq", None), P("step"), P("step"), P("step"), P(), P("cfg", None), P(), P(), P())
    return jax.shard_map(
        local, mesh=mesh, in_specs=placed, out_specs=P("step", "seq", None), check_vma=False
    )
```

profile of v0, /device:TPU:1, one launch (start us, length us, event | category | flops | bytes accessed | tf_op | source)
XLA Modules:
  0.0 609.0 jit_solution(1627151190601193763)
XLA Ops:
  12.1 5.9 fusion.70
  20.1 9.0 %all-to-all-start = ((bf16[256,3,8,1,128]{0,4,3,1,2:T(8,128)(2,1)}), bf16[256,3,8,1,128]{0,4,3,1,2:T(8,128)(2,1)}, u32[]{:S(2)}, u32[]{:S(2)}) async-start(bf16[256,3,8,1,128]{0,4,3,1,2:T(8,128)(2,1)} %copy.39), calls=%async_computation | async-start | bytes 3145728 | tf_op jit(solution)/shard_map/all_to_all | solution.py:120
  29.6 38.0 %all-to-all-done = bf16[256,3,8,1,128]{0,4,3,1,2:T(8,128)(2,1)} async-done(((bf16[256,3,8,1,128]{0,4,3,1,2:T(8,128)(2,1)}), bf16[256,3,8,1,128]{0,4,3,1,2:T(8,128)(2,1)}, u32[]{:S(2)}, u32[]{:S(2)}) %all-to-all-start) | async-done | bytes 1572896 | tf_op jit(solution)/shard_map/all_to_all | solution.py:120
  77.7 29.0 %while.48 = (s32[]{:T(128)}, bf16[4,512,2,64]{1,3,2,0:T(8,128)(2,1)S(1)}, bf16[4,512,2,64]{1,3,2,0:T(8,128)(2,1)S(1)}, bf16[2048,2,64]{0,2,1:T(8,128)(2,1)}, bf16[2048,2,64]{0,2,1:T(8,128)(2,1)}, /*index=5*/s32[]{:T(128)}) while((s32[]{:T(128)}, bf16[4,512,2,64]{1,3,2,0:T(8,128)(2,1)S(1)}, bf16[4,512,2,64]{1,3,2,0:T(8,128)(2,1)S(1)}, ...), condition=%wide.region_7.8_spmd, body=%wide.region_4.7_spmd.sunk | while | flops 815862784 | bytes 1975369 | solution.py:60
  108.7 4.2 reshape.125
  113.5 12.3 %reduce.4 = bf16[2048,128]{1,0:T(8,128)(2,1)} reduce(bf16[2048,1,1,128]{3,2,1,0:T(2,128)(2,1)S(1)} %reshape.125, bf16[]{:T(256)} %broadcast.156), dimensions={1,2}, to_apply=%reshape.125.reduce_sub_computation | reduce | bytes 1048578 | tf_op jit(solution)/shard_map/reshape | solution.py:64
  127.7 31.5 %all_to_all.60 = bf16[8,2,16384]{2,1,0:T(2,128)(2,1)} all-to-all(bf16[8,2,16384]{2,1,0:T(2,128)(2,1)} %reshape.127), channel_id=1, replica_groups=mesh['step'=16,'cfg'=2,'seq'=8] {'seq'}, dimensions={0} | all-to-all | bytes 1048576 | tf_op jit(solution)/shard_map/all_to_all | solution.py:122
  169.4 4.1 collective-permute-start
  177.9 112.5 %all-gather.5.cloned.1.call-done = f32[4096,1024]{1,0:T(8,128)} async-done(((f32[256,1024]{1,0:T(8,128)}), f32[4096,1024]{1,0:T(8,128)}) %all-gather.5.cloned.1.call-update) | async-done | bytes 16777232 | tf_op jit(solution)/shard_map/all_gather | solution.py:14
  290.4 24.2 %while.50 = (s32[]{:T(128)}, f32[256,1024]{1,0:T(8,128)S(1)}, s32[]{:T(128)}, f32[16,256,1024]{2,1,0:T(8,128)}, s32[]{:T(128)}, /*index=5*/s32[]{:T(128)}) while((s32[]{:T(128)}, f32[256,1024]{1,0:T(8,128)S(1)}, s32[]{:T(128)}, f32[16,256,1024]{2,1,0:T(8,128)}, s32[]{:T(128)}, /*index=5*/s32[]{:T(128)}) %tuple.119), condition=%wide.region_9.10_spmd.clone, body=%wide.region_8.9_spmd.clone.sunk | while | flops 786436 | bytes 3145821 | solution.py:21
  316.3 5.7 fusion.71
  324.1 6.7 %all-to-all-start.2 = ((bf16[256,3,8,1,128]{0,4,3,1,2:T(8,128)(2,1)}), bf16[256,3,8,1,128]{0,4,3,1,2:T(8,128)(2,1)}, u32[]{:S(2)}, u32[]{:S(2)}) async-start(bf16[256,3,8,1,128]{0,4,3,1,2:T(8,128)(2,1)} %copy.46), calls=%async_computation.2 | async-start | bytes 3145728 | tf_op jit(solution)/shard_map/all_to_all | solution.py:120
  330.9 38.3 %all-to-all-done.2 = bf16[256,3,8,1,128]{0,4,3,1,2:T(8,128)(2,1)} async-done(((bf16[256,3,8,1,128]{0,4,3,1,2:T(8,128)(2,1)}), bf16[256,3,8,1,128]{0,4,3,1,2:T(8,128)(2,1)}, u32[]{:S(2)}, u32[]{:S(2)}) %all-to-all-start.2) | async-done | bytes 1572896 | tf_op jit(solution)/shard_map/all_to_all | solution.py:120
  379.4 29.0 %while.49 = (s32[]{:T(128)}, bf16[4,512,2,64]{1,3,2,0:T(8,128)(2,1)S(1)}, bf16[4,512,2,64]{1,3,2,0:T(8,128)(2,1)S(1)}, bf16[2048,2,64]{0,2,1:T(8,128)(2,1)}, bf16[2048,2,64]{0,2,1:T(8,128)(2,1)}, /*index=5*/s32[]{:T(128)}) while((s32[]{:T(128)}, bf16[4,512,2,64]{1,3,2,0:T(8,128)(2,1)S(1)}, bf16[4,512,2,64]{1,3,2,0:T(8,128)(2,1)S(1)}, ...), condition=%wide.region_17.18_spmd, body=%wide.region_14.17_spmd.sunk | while | flops 815862784 | bytes 1975369 | solution.py:60
  382.7 3.9 fusion.137
  390.0 3.9 fusion.137
  397.2 3.9 fusion.137
  404.5 3.9 fusion.137
  410.4 4.2 reshape.126
  414.6 12.3 %reduce.5 = bf16[2048,128]{1,0:T(8,128)(2,1)} reduce(bf16[2048,1,1,128]{3,2,1,0:T(2,128)(2,1)S(1)} %reshape.126, bf16[]{:T(256)} %broadcast.156), dimensions={1,2}, to_apply=%reshape.126.reduce_sub_computation | reduce | bytes 1048578 | tf_op jit(solution)/shard_map/reshape | solution.py:64
  428.9 18.8 %all_to_all.61 = bf16[8,2,16384]{2,1,0:T(2,128)(2,1)} all-to-all(bf16[8,2,16384]{2,1,0:T(2,128)(2,1)} %reshape.129), channel_id=1, replica_groups=mesh['step'=16,'cfg'=2,'seq'=8] {'seq'}, dimensions={0} | all-to-all | bytes 1048576 | tf_op jit(solution)/shard_map/all_to_all | solution.py:122
  457.1 4.1 collective-permute-start.1
  464.1 110.8 %all-gather.7.cloned.1.call-done = f32[4096,1024]{1,0:T(8,128)} async-done(((f32[256,1024]{1,0:T(8,128)}), f32[4096,1024]{1,0:T(8,128)}) %all-gather.7.cloned.1.call-update) | async-done | bytes 16777232 | tf_op jit(solution)/shard_map/all_gather | solution.py:14
  574.9 24.2 %while.51 = (s32[]{:T(128)}, f32[256,1024]{1,0:T(8,128)S(1)}, s32[]{:T(128)}, f32[16,256,1024]{2,1,0:T(8,128)}, s32[]{:T(128)}, /*index=5*/s32[]{:T(128)}) while((s32[]{:T(128)}, f32[256,1024]{1,0:T(8,128)S(1)}, s32[]{:T(128)}, f32[16,256,1024]{2,1,0:T(8,128)}, s32[]{:T(128)}, /*index=5*/s32[]{:T(128)}) %tuple.120), condition=%wide.region_19.20_spmd.clone, body=%wide.region_18.19_spmd.clone.sunk | while | flops 786436 | bytes 3145821 | solution.py:21
  (114 shorter events, 157.9 us)
Async XLA Ops:
  6.5 160.3 %copy-start = (bf16[1024,1024]{1,0:T(8,128)(2,1)S(1)}, bf16[1024,1024]{1,0:T(8,128)(2,1)}, u32[]{:S(2)}) copy-start(bf16[1024,1024]{1,0:T(8,128)(2,1)} %param.24) | copy-start | bytes 6291460
  12.1 6.2 %copy-start.4 = (f32[16]{0:T(128)S(1)}, f32[16]{0:T(128)}, u32[]{:S(2)}) copy-start(f32[16]{0:T(128)} %param.25) | copy-start | bytes 196
  20.1 47.4 %all-to-all-start = ((bf16[256,3,8,1,128]{0,4,3,1,2:T(8,128)(2,1)}), bf16[256,3,8,1,128]{0,4,3,1,2:T(8,128)(2,1)}, u32[]{:S(2)}, u32[]{:S(2)}) async-start(bf16[256,3,8,1,128]{0,4,3,1,2:T(8,128)(2,1)} %copy.39), calls=%async_computation | async-start | bytes 3145728 | tf_op jit(solution)/shard_map/all_to_all | solution.py:120
  29.1 261.3 %all-gather.5.cloned.1.call-start = ((), (), s32[]{:S(2)}) async-start(), calls=%async_computation.4 | async-start | bytes 17825792 | tf_op jit(solution)/shard_map/all_gather | solution.py:14
  127.7 47.6 %copy-start.1 = (f32[256,1024]{1,0:T(8,128)S(1)}, f32[256,1024]{1,0:T(8,128)}, u32[]{:S(2)}) copy-start(f32[256,1024]{1,0:T(8,128)} %param.17) | copy-start | bytes 3145732
  169.4 5.9 collective-permute-start
  316.0 6.0 copy-start.2
  324.1 45.1 %all-to-all-start.2 = ((bf16[256,3,8,1,128]{0,4,3,1,2:T(8,128)(2,1)}), bf16[256,3,8,1,128]{0,4,3,1,2:T(8,128)(2,1)}, u32[]{:S(2)}, u32[]{:S(2)}) async-start(bf16[256,3,8,1,128]{0,4,3,1,2:T(8,128)(2,1)} %copy.46), calls=%async_computation.2 | async-start | bytes 3145728 | tf_op jit(solution)/shard_map/all_to_all | solution.py:120
  330.8 244.1 %all-gather.7.cloned.1.call-start = ((), (), s32[]{:S(2)}) async-start(), calls=%async_computation.5 | async-start | bytes 17825792 | tf_op jit(solution)/shard_map/all_gather | solution.py:14
  428.9 33.9 %copy-start.3 = (f32[256,1024]{1,0:T(8,128)S(1)}, f32[256,1024]{1,0:T(8,128)}, u32[]{:S(2)}) copy-start(f32[256,1024]{1,0:T(8,128)} %copy-done.2) | copy-start | bytes 3145732
  457.1 5.7 collective-permute-start.1
Sparse Core Ops, SparseCore 0:
  178.0 112.3 all-gather.4
  464.3 110.5 all-gather.6
where the time goes:
time: 616 us; the launch traced here: 609 us
  waiting for transfers between devices  302 us (49%)
  other arithmetic  85.7 us (14%)
  matrix products  74.8 us (12%)
  local copies, waits for them, and re-layouts  55.1 us (9%)
  blocking collectives  50.4 us (8%)
  starting transfers between devices  24.4 us (4%)
  between operations  16 us (3%)
    all_gather x2, waiting for transfers between devices, entering(): pieces = lax.all_gather(value, axis)  223 us
    all_to_all x2, waiting for transfers between devices, local(): lax.all_to_all(packed, 'seq', split_axis=2, concat_axis=0, tiled=True)  76.3 us
    all_to_all x2, blocking collectives, local(): lax.all_to_all(attended, 'seq', split_axis=0, concat_axis=1, tiled=True)  50.4 us
    select_n x30, other arithmetic, turn(): return jnp.where(position < mine, longer, total)  47.7 us
    dot_general x8, matrix products, block_attention(): jnp.einsum('hqk,khd->qhd', weights, value_rows, preferred_element_type=jn...  31.3 us
    sub x8, matrix products, block_attention(): powers = jnp.exp(scores - row_max)  26.5 us
    reshape x2, other arithmetic, attend_pairs(): return result.reshape(frames, 1, pair_count, 2 * subspace_dimension)  24.6 us
    all_to_all x2, starting transfers between devices, local(): lax.all_to_all(packed, 'seq', split_axis=2, concat_axis=0, tiled=True)  15.7 us
  transfers between devices with their start and end apart: 6, of which 6 were waited for; matrix products, arithmetic and copies ran while one was open for 0% of the time, Pallas kernels for 0%

commit v1 on v0

v1 whole, which is shorter than its diff:
```python
import math

import jax
import jax.numpy as jnp
from jax import lax
from jax.experimental import pallas as pl
from jax.experimental.pallas import tpu as pltpu
from jax.sharding import PartitionSpec as P

MESH = pl.DeviceIdType.MESH
F32 = jnp.float32
BF16 = jnp.bfloat16
LOG2E = 1.4426950408889634

WIDTH = 1024
FRAMES = 2048
CHUNK = 128
TILE = 256
RING = 8
STEPS = 16
COLUMN = 16


def remote(src, dst, send_sem, recv_sem, device):
    return pltpu.make_async_remote_copy(
        src_ref=src,
        dst_ref=dst,
        send_sem=send_sem,
        recv_sem=recv_sem,
        device_id=device,
        device_id_type=MESH,
    )


def fold(rows):
    half = WIDTH // 2
    return jnp.concatenate([rows[:, :, :half], rows[:, :, half:]], axis=1).astype(BF16)


def unfold(tiles):
    wide = tiles.astype(F32)
    return jnp.concatenate([wide[:, :8], wide[:, 8:]], axis=2)


def layer_norm(rows):
    average = jnp.mean(rows, axis=-1, keepdims=True)
    centred = rows - average
    variance = jnp.mean(centred * centred, axis=-1, keepdims=True)
    return centred * lax.rsqrt(variance + 1e-06)


def kernel(
    clip_ref,
    ordinal_ref,
    strength_ref,
    increment_ref,
    table_ref,
    pair_ref,
    w_in_ref,
    w_merge_ref,
    sharp_ref,
    out_ref,
    xall,
    w_raw,
    w_mod,
    w_out,
    bias,
    qb,
    kb,
    vb,
    acc,
    ob,
    att,
    sb,
    rb,
    nb,
    nr,
    fin,
    states,
    gates,
    incs,
    local_sem,
    maj_send,
    min_send,
    d2d_send,
    ring_recv,
    a2a_send,
    a2a_recv,
    s_send,
    s_recv,
    n_send,
    n_recv,
    inc_send,
    inc_recv,
    pair_send,
    pair_recv,
):
    k = lax.axis_index("step")
    c = lax.axis_index("cfg")
    z = lax.axis_index("seq")
    other = 1 - c
    sign = 1 - 2 * c
    mine = 2 * z + c

    barrier = pltpu.get_barrier_semaphore()

    def greet(o, carry):
        e = lax.rem(mine + o, COLUMN)
        pl.semaphore_signal(
            barrier, inc=1, device_id={"seq": e // 2, "cfg": lax.rem(e, 2)}, device_id_type=MESH
        )
        pl.semaphore_signal(
            barrier, inc=1, device_id={"step": lax.rem(k + o, STEPS)}, device_id_type=MESH
        )
        return carry

    lax.fori_loop(1, COLUMN, greet, 0)

    loads = []
    for part in range(3):
        columns = pl.ds(pl.multiple_of(part * WIDTH + z * 128, 128), 128)
        loads.append(
            pltpu.make_async_copy(
                w_in_ref.at[:, columns], w_raw.at[part], local_sem.at[part]
            )
        )
    loads.append(pltpu.make_async_copy(w_merge_ref, w_out, local_sem.at[3]))
    for load in loads:
        load.start()

    own_rows = pl.ds(pl.multiple_of(c * CHUNK, CHUNK), CHUNK)
    xall[0, mine] = layer_norm(clip_ref[own_rows, :]).astype(BF16)

    lane = lax.broadcasted_iota(jnp.int32, (1, 128), 1)
    first_head = lane < 64

    pl.semaphore_wait(barrier, 2 * (COLUMN - 1))

    def slot(zz, cc):
        return 2 * zz + cc

    def ring(t, index, send_sem, zz):
        block = xall.at[t, index]
        return remote(block, block, send_sem, ring_recv.at[t, index], {"seq": zz})

    def across(t, index, i):
        block = xall.at[t, index]
        return remote(block, block, d2d_send.at[t, i], ring_recv.at[t, index], {"cfg": other})

    z_major = lax.rem(z + sign + RING, RING)
    z_minor = lax.rem(z - sign + RING, RING)

    def begin(t):
        ring(t, mine, maj_send.at[t, 0], z_major).start()
        ring(t, mine, min_send.at[t, 0], z_minor).start()
        across(t, mine, 0).start()

    begin(0)

    chosen = (
        lax.broadcasted_iota(jnp.int32, (16, table_ref.shape[0]), 1) == ordinal_ref[0]
    ).astype(BF16)
    affine = jnp.dot(chosen, table_ref[...], preferred_element_type=F32)[:8] + pair_ref[
        ...
    ].astype(F32)
    shift = affine[:, :WIDTH]
    scale_now = strength_ref[0]
    step_now = increment_ref[0]
    share = jnp.where(c == 0, scale_now, 1.0 - scale_now) * step_now
    gates[c] = affine[:, 2 * WIDTH :] * share
    incs[k] = jnp.full((8, 128), step_now, F32)
    gate_copy = remote(
        gates.at[c], gates.at[c], pair_send.at[0], pair_recv.at[0], {"cfg": other}
    )
    gate_copy.start()

    def inc_copy(o):
        return remote(
            incs.at[k],
            incs.at[k],
            inc_send.at[o],
            inc_recv.at[k],
            {"step": lax.rem(k + o, STEPS)},
        )

    def send_inc(o, carry):
        inc_copy(o).start()
        return carry

    lax.fori_loop(1, STEPS, send_inc, 0)

    scale_column = jnp.transpose(
        jnp.broadcast_to(1.0 + affine[:1, WIDTH : 2 * WIDTH], (128, WIDTH))
    )
    shift_high = shift.astype(BF16)
    shift_low = shift - shift_high.astype(F32)
    shift_parts = jnp.concatenate([shift_high.astype(F32), shift_low], axis=0).astype(BF16)
    for part in range(3):
        loads[part].wait()
        raw = w_raw[part]
        both = jnp.dot(shift_parts, raw, preferred_element_type=F32)
        bias[:, part * 128 : (part + 1) * 128] = both[:8] + both[8:]
        w_mod[:, part * 128 : (part + 1) * 128] = (raw.astype(F32) * scale_column).astype(BF16)
    ones = jnp.ones((1, 128), F32)
    for h in range(2):
        mask = first_head if h == 0 else jnp.logical_not(first_head)
        vb[h, :, 128:] = jnp.broadcast_to(jnp.where(mask, ones, 0.0), (FRAMES, 128)).astype(BF16)
    q_scale = jnp.where(first_head, sharp_ref[2 * z], sharp_ref[2 * z + 1]) * (
        LOG2E / math.sqrt(64.0)
    )
    same_head = (
        (lax.broadcasted_iota(jnp.int32, (128, 128), 0) < 64)
        == (lax.broadcasted_iota(jnp.int32, (128, 128), 1) < 64)
    ).astype(F32).astype(BF16)

    def project(t, start, slots):
        rows = len(slots) * CHUNK
        block = jnp.concatenate([xall[t, s] for s in slots], axis=0)
        qkv = jnp.dot(block, w_mod[...], preferred_element_type=F32) + bias[:1, :]
        here = pl.ds(start, rows)

        def normalize(values):
            squares = jnp.dot(
                (values * values).astype(BF16), same_head, preferred_element_type=F32
            )
            return values * lax.rsqrt(squares * (1.0 / 64.0) + 1e-06)

        qb[here, :] = (normalize(qkv[:, :128]) * q_scale).astype(BF16)
        keys = normalize(qkv[:, 128:256])
        values = qkv[:, 256:]
        for h in range(2):
            mask = first_head if h == 0 else jnp.logical_not(first_head)
            kb[h, here, :] = jnp.where(mask, keys, 0.0).astype(BF16)
            vb[h, here, :128] = jnp.where(mask, values, 0.0).astype(BF16)

    def attend(q_start, low, high, total):
        q = qb[pl.ds(q_start, TILE), :]
        for j in range(low, high, 256):
            for h in range(2):
                scores = lax.dot_general(
                    q, kb[h, j : j + 256, :], (((1,), (1,)), ((), ())), preferred_element_type=F32
                )
                powers = jnp.exp2(scores).astype(BF16)
                total = total + jnp.dot(
                    powers, vb[h, j : j + 256, :], preferred_element_type=F32
                )
        return total

    zero = jnp.zeros((TILE, 256), F32)

    def older(low, high):
        def tile(i, carry):
            start = pl.multiple_of(i * TILE, TILE)
            rows = pl.ds(start, TILE)
            acc[rows, :] = attend(start, low, high, acc[rows, :])
            return carry

        lax.fori_loop(0, low // TILE, tile, 0)

    def newer(low, high):
        def tile(i, carry):
            start = pl.multiple_of(i * TILE, TILE)
            acc[pl.ds(start, TILE), :] = attend(start, 0, high, zero)
            return carry

        lax.fori_loop(low // TILE, high // TILE, tile, 0)

    def place(i):
        if i % 2:
            return lax.rem(z - (i + 1) // 2 * sign + RING, RING)
        return lax.rem(z + i // 2 * sign + RING, RING)

    def result_copy(t, i, side):
        target = {"seq": place(i), "cfg": c if side == 0 else other}
        return remote(
            ob.at[t, 2 * i + side],
            att.at[t, c, z],
            a2a_send.at[t, 2 * i + side],
            a2a_recv.at[t, mine],
            target,
        )

    def gather_and_attend(t):
        ring(t, slot(z, other), maj_send.at[t, 0], z_major).wait_recv()
        project(t, 0, [mine, slot(z, other)])
        newer(0, TILE)
        for i in range(1, 5):
            behind = lax.rem(z - i * sign + RING, RING)
            ahead = lax.rem(z + i * sign + RING, RING)
            ring(t, slot(behind, c), maj_send.at[t, 0], z_major).wait_recv()
            if i < 4:
                ring(t, slot(behind, c), maj_send.at[t, i], z_major).start()
            across(t, slot(behind, c), i).start()
            if i < 4:
                ring(t, slot(ahead, c), min_send.at[t, 0], z_minor).wait_recv()
                if i < 3:
                    ring(t, slot(ahead, c), min_send.at[t, i], z_minor).start()
                across(t, slot(ahead, c), 4 + i).start()
            across(t, slot(behind, other), 0).wait_recv()
            slots = [slot(behind, c), slot(behind, other)]
            if i < 4:
                across(t, slot(ahead, other), 0).wait_recv()
                slots += [slot(ahead, c), slot(ahead, other)]
            low = TILE + 2 * TILE * (i - 1)
            high = low + len(slots) * CHUNK
            project(t, low, slots)
            if i < 4:
                older(low, high)
                newer(low, high)
        last = FRAMES - TILE
        for i in (5, 6, 3, 4, 1, 2, 7, 0):
            if i == 7:
                total = attend(last, 0, FRAMES, zero)
            else:
                total = attend(i * TILE, last, FRAMES, acc[i * TILE : (i + 1) * TILE, :])
            result = (total[:, :128] / total[:, 128:]).astype(BF16)
            for side in range(2):
                piece = result[side * CHUNK : (side + 1) * CHUNK]
                if i == 0 and side == 0:
                    att[t, c, z] = piece
                else:
                    ob[t, 2 * i + side] = piece
                    result_copy(t, i, side).start()

    def clip_rows():
        return clip_ref[pl.ds(pl.multiple_of(c * CHUNK + k * 8, 8), 8), :]

    def peer_copy(src, dst, send, recv, t, o):
        target = lax.rem(k + o, STEPS)
        return remote(
            src.at[t, target], dst.at[t, k], send.at[t, o], recv.at[t, k], {"step": target}
        )

    def exchange(src, dst, send, recv, t):
        def start(o, carry):
            peer_copy(src, dst, send, recv, t, o).start()
            return carry

        lax.fori_loop(1, STEPS, start, 0)
        dst[t, k] = src[t, k]

        def arrive(o, carry):
            source = lax.rem(k + o, STEPS)
            remote(
                src.at[t, source],
                dst.at[t, source],
                send.at[t, o],
                recv.at[t, source],
                {"step": source},
            ).wait_recv()
            return carry

        lax.fori_loop(1, STEPS, arrive, 0)

    def merge(t):
        def arrive(o, carry):
            e = lax.rem(mine + o, COLUMN)
            zz, cc = e // 2, lax.rem(e, 2)
            remote(
                ob.at[t, 0],
                att.at[t, cc, zz],
                a2a_send.at[t, 0],
                a2a_recv.at[t, e],
                {"seq": zz, "cfg": cc},
            ).wait_recv()
            return carry

        lax.fori_loop(1, COLUMN, arrive, 0)
        attended = jnp.concatenate(
            [
                jnp.concatenate([att[t, cc, zz] for zz in range(RING)], axis=1)
                for cc in range(2)
            ],
            axis=0,
        )
        projected = jnp.dot(attended, w_out[...], preferred_element_type=F32)
        terms = projected[:CHUNK] * gates[0, :1, :] + projected[CHUNK:] * gates[1, :1, :]
        sb[t] = fold(terms.reshape(STEPS, 8, WIDTH))
        exchange(sb, rb, s_send, s_recv, t)
        return unfold(rb[t])

    def increment(j):
        return jnp.concatenate([incs[j]] * (WIDTH // 128), axis=1)

    gather_and_attend(0)
    loads[3].wait()
    gate_copy_back = remote(
        gates.at[other], gates.at[other], pair_send.at[0], pair_recv.at[0], {"cfg": other}
    )
    gate_copy_back.wait_recv()

    def inc_arrive(o, carry):
        source = lax.rem(k + o, STEPS)
        remote(
            incs.at[source],
            incs.at[source],
            inc_send.at[o],
            inc_recv.at[source],
            {"step": source},
        ).wait_recv()
        return carry

    lax.fori_loop(1, STEPS, inc_arrive, 0)

    terms = merge(0)
    start_rows = clip_rows()
    total = jnp.zeros_like(start_rows)
    for j in range(STEPS):
        states[j] = start_rows + total
        total = total + (increment(j) * start_rows + terms[j])
    nb[0] = fold(layer_norm(states[...]))
    exchange(nb, nr, n_send, n_recv, 0)
    xall[1, mine] = unfold(nr[0]).reshape(CHUNK, WIDTH).astype(BF16)

    begin(1)
    gather_and_attend(1)
    terms = merge(1)
    total = jnp.zeros_like(start_rows)
    drifts = []
    for j in range(STEPS):
        total = total + (increment(j) * states[j] + terms[j])
        drifts.append(total)
    nb[1] = fold(jnp.stack(drifts, axis=0))
    exchange(nb, nr, n_send, n_recv, 1)
    final_copy = remote(nr.at[1], fin, pair_send.at[1], pair_recv.at[1], {"cfg": other})
    final_copy.start()
    out_ref[own_rows, :] = clip_ref[own_rows, :] + unfold(nr[1]).reshape(CHUNK, WIDTH)
    final_copy.wait_recv()
    far_rows = pl.ds(pl.multiple_of(other * CHUNK, CHUNK), CHUNK)
    out_ref[far_rows, :] = clip_ref[far_rows, :] + unfold(fin[...]).reshape(CHUNK, WIDTH)

    final_copy.wait_send()
    gate_copy.wait_send()

    def inc_left(o, carry):
        inc_copy(o).wait_send()
        for t in range(2):
            peer_copy(sb, rb, s_send, s_recv, t, o).wait_send()
            peer_copy(nb, nr, n_send, n_recv, t, o).wait_send()
        return carry

    lax.fori_loop(1, STEPS, inc_left, 0)
    for t in range(2):
        for i in range(8):
            across(t, mine, i).wait_send()
            for side in range(2):
                if i or side:
                    result_copy(t, i, side).wait_send()
        for i in range(4):
            ring(t, mine, maj_send.at[t, i], z_major).wait_send()
        for i in range(3):
            ring(t, mine, min_send.at[t, i], z_minor).wait_send()


def local(clip, ordinal, strength, increment, table, pair, w_in, w_merge, sharp):
    vmem = pl.BlockSpec(memory_space=pltpu.VMEM)
    smem = pl.BlockSpec(memory_space=pltpu.SMEM)
    anywhere = pl.BlockSpec(memory_space=pl.ANY)
    dma = pltpu.SemaphoreType.DMA
    out = pl.pallas_call(
        kernel,
        out_shape=jax.ShapeDtypeStruct(clip.shape, F32),
        in_specs=[vmem, smem, smem, smem, vmem, vmem, anywhere, anywhere, smem],
        out_specs=vmem,
        scratch_shapes=[
            pltpu.VMEM((2, COLUMN, CHUNK, WIDTH), BF16),
            pltpu.VMEM((3, WIDTH, 128), BF16),
            pltpu.VMEM((WIDTH, 384), BF16),
            pltpu.VMEM((WIDTH, WIDTH), BF16),
            pltpu.VMEM((8, 384), F32),
            pltpu.VMEM((FRAMES, 128), BF16),
            pltpu.VMEM((2, FRAMES, 128), BF16),
            pltpu.VMEM((2, FRAMES, 256), BF16),
            pltpu.VMEM((FRAMES, 256), F32),
            pltpu.VMEM((2, COLUMN, CHUNK, 128), BF16),
            pltpu.VMEM((2, 2, RING, CHUNK, 128), BF16),
            pltpu.VMEM((2, STEPS, 16, 512), BF16),
            pltpu.VMEM((2, STEPS, 16, 512), BF16),
            pltpu.VMEM((2, STEPS, 16, 512), BF16),
            pltpu.VMEM((2, STEPS, 16, 512), BF16),
            pltpu.VMEM((STEPS, 16, 512), BF16),
            pltpu.VMEM((STEPS, 8, WIDTH), F32),
            pltpu.VMEM((2, 8, WIDTH), F32),
            pltpu.VMEM((STEPS, 8, 128), F32),
            dma((4,)),
            dma((2, 4)),
            dma((2, 3)),
            dma((2, 8)),
            dma((2, COLUMN)),
            dma((2, COLUMN)),
            dma((2, COLUMN)),
            dma((2, STEPS)),
            dma((2, STEPS)),
            dma((2, STEPS)),
            dma((2, STEPS)),
            dma((STEPS,)),
            dma((STEPS,)),
            dma((2,)),
            dma((2,)),
        ],
        compiler_params=pltpu.CompilerParams(
            collective_id=0, has_side_effects=True, vmem_limit_bytes=56 * 2**20
        ),
    )(clip, ordinal, strength, increment, table, pair, w_in, w_merge, sharp)
    return out[None]


def solution(mesh):
    placed = (P("seq", None), P("step"), P("step"), P("step"), P(), P("cfg", None), P(), P(), P())
    return jax.shard_map(
        local, mesh=mesh, in_specs=placed, out_specs=P("step", "seq", None), check_vma=False
    )
```

time: 616 us -> 139 us (0.23); the launches traced: 609 us -> 139 us
  waiting for transfers between devices: 302 us -> 0 us
  Pallas kernels: 0 us -> 135 us
  other arithmetic: 85.7 us -> 0 us
  matrix products: 74.8 us -> 0 us
  local copies, waits for them, and re-layouts: 55.1 us -> 2.31 us
  blocking collectives: 50.4 us -> 0 us
  starting transfers between devices: 24.4 us -> 0 us
  between operations: 16 us -> 1.95 us
    all_gather x2 -> x0, waiting for transfers between devices: 223 us -> none  [entering(): pieces = lax.all_gather(value, axis)]
    pallas_call x0 -> x1, Pallas kernels: none -> 135 us  [local(): pl.pallas_call(kernel, out_shape=jax.ShapeDtypeStruct(clip.shape, F32), i...]
    all_to_all x2 -> x0, waiting for transfers between devices: 76.3 us -> none  [local(): lax.all_to_all(packed, 'seq', split_axis=2, concat_axis=0, tiled=True)]
    all_to_all x2 -> x0, blocking collectives: 50.4 us -> none  [local(): lax.all_to_all(attended, 'seq', split_axis=0, concat_axis=1, tiled=True)]
    dot_general x13 -> x0, matrix products: 48.3 us -> none  [the longest x8 31.3 us: block_attention(): jnp.einsum('hqk,khd->qhd', weights, value_rows, preferred_element_type=jn...]
    select_n x30 -> x0, other arithmetic: 47.7 us -> none  [turn(): return jnp.where(position < mine, longer, total)]
    sub x8 -> x0, matrix products: 26.5 us -> none  [block_attention(): powers = jnp.exp(scores - row_max)]
    reshape x2 -> x0, other arithmetic: 24.6 us -> none  [attend_pairs(): return result.reshape(frames, 1, pair_count, 2 * subspace_dimension)]
  transfers between devices with their start and end apart: 6 -> 0, of which waited for: 6 -> 0; matrix products, arithmetic and copies ran while one was open for 0% -> 0% of each run, Pallas kernels for 0% -> 0%
where the time goes in v1:
time: 139 us
  Pallas kernels  135 us (97%)
  local copies, waits for them, and re-layouts  2.31 us (2%)
  between operations  1.95 us (1%)
    pallas_call x1, Pallas kernels, local(): pl.pallas_call(kernel, out_shape=jax.ShapeDtypeStruct(clip.shape, F32), i...  135 us

profile of v1, /device:TPU:1, one launch (start us, length us, event | category | flops | bytes accessed | tf_op | source)
XLA Modules:
  0.0 139.2 jit_solution(14013686266213219082)
XLA Ops:
  1.9 135.0 %shard_map.91 = f32[256,1024]{1,0:T(8,128)} custom-call(f32[256,1024]{1,0:T(8,128)} %clip_ref.1, s32[1]{0:T(128)S(6)} %copy.11.ordinal_ref, f32[1]{0:T(128)S(6)} %copy.12.strength_ref, f32[1]{0:T(128)S(6)} %copy.13.increment_ref, bf16[50,3072]{1,0:T(8,128)(2,1)} %table_ref.1, bf16[1,3072]{1,0:T(2,128)(2,1)} %pair_ref.1, bf16[1024,3072]{1,0:T(8,128)(2,1)} %w_in_ref.1, ...), custom_call_target="tpu_custom_call" | custom-call | tf_op jit(solution)/shard_map/pallas_call | solution.py:460
  136.9 2.3 %copy.14 = f32[1,256,1024]{2,1,0:T(8,128)} copy(f32[1,256,1024]{2,1,0:T(8,128)} %bitcast.1) | data formatting | bytes 2097152

commit v2 on v1

--- a/solution.py
+++ b/solution.py
@@ -14,6 +14,7 @@
 
 WIDTH = 1024
 FRAMES = 2048
+HALF = 64
 CHUNK = 128
 TILE = 256
 RING = 8
@@ -84,6 +85,10 @@
     min_send,
     d2d_send,
     ring_recv,
+    far_send,
+    far_recv,
+    plane_send,
+    plane_recv,
     a2a_send,
     a2a_recv,
     s_send,
@@ -129,33 +134,10 @@
         load.start()
 
     own_rows = pl.ds(pl.multiple_of(c * CHUNK, CHUNK), CHUNK)
-    xall[0, mine] = layer_norm(clip_ref[own_rows, :]).astype(BF16)
+    xall[0, 0, c] = layer_norm(clip_ref[own_rows, :]).astype(BF16)
 
     lane = lax.broadcasted_iota(jnp.int32, (1, 128), 1)
     first_head = lane < 64
-
-    pl.semaphore_wait(barrier, 2 * (COLUMN - 1))
-
-    def slot(zz, cc):
-        return 2 * zz + cc
-
-    def ring(t, index, send_sem, zz):
-        block = xall.at[t, index]
-        return remote(block, block, send_sem, ring_recv.at[t, index], {"seq": zz})
-
-    def across(t, index, i):
-        block = xall.at[t, index]
-        return remote(block, block, d2d_send.at[t, i], ring_recv.at[t, index], {"cfg": other})
-
-    z_major = lax.rem(z + sign + RING, RING)
-    z_minor = lax.rem(z - sign + RING, RING)
-
-    def begin(t):
-        ring(t, mine, maj_send.at[t, 0], z_major).start()
-        ring(t, mine, min_send.at[t, 0], z_minor).start()
-        across(t, mine, 0).start()
-
-    begin(0)
 
     chosen = (
         lax.broadcasted_iota(jnp.int32, (16, table_ref.shape[0]), 1) == ordinal_ref[0]
@@ -169,26 +151,6 @@
     share = jnp.where(c == 0, scale_now, 1.0 - scale_now) * step_now
     gates[c] = affine[:, 2 * WIDTH :] * share
     incs[k] = jnp.full((8, 128), step_now, F32)
-    gate_copy = remote(
-        gates.at[c], gates.at[c], pair_send.at[0], pair_recv.at[0], {"cfg": other}
-    )
-    gate_copy.start()
-
-    def inc_copy(o):
-        return remote(
-            incs.at[k],
-            incs.at[k],
-            inc_send.at[o],
-            inc_recv.at[k],
-            {"step": lax.rem(k + o, STEPS)},
-        )
-
-    def send_inc(o, carry):
-        inc_copy(o).start()
-        return carry
-
-    lax.fori_loop(1, STEPS, send_inc, 0)
-
     scale_column = jnp.transpose(
         jnp.broadcast_to(1.0 + affine[:1, WIDTH : 2 * WIDTH], (128, WIDTH))
     )
@@ -213,9 +175,133 @@
         == (lax.broadcasted_iota(jnp.int32, (128, 128), 1) < 64)
     ).astype(F32).astype(BF16)
 
+    pl.semaphore_wait(barrier, 2 * (COLUMN - 1))
+
+    def rel(offset):
+        return lax.rem(offset * sign + RING, RING)
+
+    def half_rows(h):
+        return pl.ds(h * HALF, HALF)
+
+    def at(t, offset, core, h):
+        return xall.at[t, rel(offset), core, half_rows(h)]
+
+    z_major = lax.rem(z + sign + RING, RING)
+    z_minor = lax.rem(z - sign + RING, RING)
+
+    def major(t, i, h):
+        return remote(
+            at(t, -i, c, h),
+            at(t, -(i + 1), c, h),
+            maj_send.at[t, i, h],
+            ring_recv.at[t, rel(-(i + 1)), c, h],
+            {"seq": z_major},
+        )
+
+    def minor(t, i, h):
+        return remote(
+            at(t, i, c, h),
+            at(t, i + 1, c, h),
+            min_send.at[t, i, h],
+            ring_recv.at[t, rel(i + 1), c, h],
+            {"seq": z_minor},
+        )
+
+    def across(t, offset, h, core):
+        block = at(t, offset, core, h)
+        return remote(
+            block,
+            block,
+            d2d_send.at[t, rel(offset), h],
+            ring_recv.at[t, rel(offset), core, h],
+            {"cfg": other},
+        )
+
+    def begin(t):
+        for h in range(2):
+            major(t, 0, h).start()
+            minor(t, 0, h).start()
+        for h in range(2):
+            across(t, 0, h, c).start()
+
+    def onward(t, i, h, hops):
+        major(t, i - 1, h).wait_recv()
+        if i < hops:
+            major(t, i, h).start()
+        across(t, -i, h, c).start()
+        if i < 4:
+            minor(t, i - 1, h).wait_recv()
+            if i < min(hops, 3):
+                minor(t, i, h).start()
+            across(t, i, h, c).start()
+
+    def other_half_came(t, offset):
+        for h in range(2):
+            across(t, offset, h, other).wait_recv()
+
+    piece = (
+        pl.ds(pl.multiple_of(k // 8 * HALF, HALF), HALF),
+        pl.ds(pl.multiple_of(lax.rem(k, 8) * 128, 128), 128),
+    )
+
+    def far_copy(i):
+        return remote(
+            xall.at[0, 0, c, piece[0], piece[1]],
+            xall.at[0, 3 + i, c, piece[0], piece[1]],
+            far_send.at[i],
+            far_recv.at[i],
+            {"seq": lax.rem(z + 5 - i, RING)},
+        )
+
+    def plane_block(step):
+        return xall.at[
+            0,
+            pl.ds(3, 3),
+            c,
+            pl.ds(pl.multiple_of(step // 8 * HALF, HALF), HALF),
+            pl.ds(pl.multiple_of(lax.rem(step, 8) * 128, 128), 128),
+        ]
+
+    def plane_copy(o):
+        return remote(
+            plane_block(k),
+            plane_block(k),
+            plane_send.at[o],
+            plane_recv.at[k],
+            {"step": lax.rem(k + o, STEPS)},
+        )
+
+    def plane_half(core, h):
+        return xall.at[0, pl.ds(3, 3), core, half_rows(h)]
+
+    def plane_across(core, h):
+        block = plane_half(core, h)
+        return remote(block, block, far_send.at[3 + h], far_recv.at[3 + h], {"cfg": other})
+
+    begin(0)
+    for i in range(3):
+        far_copy(i).start()
+    gate_copy = remote(
+        gates.at[c], gates.at[c], pair_send.at[0], pair_recv.at[0], {"cfg": other}
+    )
+    gate_copy.start()
+
+    def inc_copy(o):
+        return remote(
+            incs.at[k],
+            incs.at[k],
+            inc_send.at[o],
+            inc_recv.at[k],
+            {"step": lax.rem(k + o, STEPS)},
+        )
+
+    def send_inc(o, carry):
+        inc_copy(o).start()
+        return carry
+
     def project(t, start, slots):
         rows = len(slots) * CHUNK
-        block = jnp.concatenate([xall[t, s] for s in slots], axis=0)
+        block = jnp.concatenate([xall[t, slab, core] for slab, core in slots], axis=0)
         qkv = jnp.dot(block, w_mod[...], preferred_element_type=F32) + bias[:1, :]
         here = pl.ds(start, rows)
 
@@ -265,13 +351,15 @@
 
         lax.fori_loop(low // TILE, high // TILE, tile, 0)
 
-    def place(i):
-        if i % 2:
-            return lax.rem(z - (i + 1) // 2 * sign + RING, RING)
-        return lax.rem(z + i // 2 * sign + RING, RING)
+    def place(t, i):
+        if t == 0 and i in (3, 4, 5):
+            return i
+        if t == 0 and i > 5:
+            i = i - 3
+        return rel(-(i + 1) // 2 if i % 2 else i // 2)
 
     def result_copy(t, i, side):
-        target = {"seq": place(i), "cfg": c if side == 0 else other}
+        target = {"seq": lax.rem(z + place(t, i), RING), "cfg": c if side == 0 else other}
         return remote(
             ob.at[t, 2 * i + side],
             att.at[t, c, z],
@@ -280,37 +368,78 @@
             target,
         )
 
-    def gather_and_attend(t):
-        ring(t, slot(z, other), maj_send.at[t, 0], z_major).wait_recv()
-        project(t, 0, [mine, slot(z, other)])
+    def both(slab):
+        return [(slab, c), (slab, other)]
+
+    def gather_first():
+        other_half_came(0, 0)
+        project(0, 0, both(0))
         newer(0, TILE)
+        for i in range(3):
+            far_copy(i).wait_recv()
+
+        def spread(o, carry):
+            plane_copy(o).start()
+            return carry
+
+        lax.fori_loop(1, STEPS, spread, 0)
+        lax.fori_loop(1, STEPS, send_inc, 0)
+        onward(0, 1, 0, 2)
+        onward(0, 1, 1, 2)
+        other_half_came(0, -1)
+        other_half_came(0, 1)
+        project(0, 256, both(rel(-1)) + both(rel(1)))
+        older(256, 768)
+        onward(0, 2, 0, 2)
+        newer(256, 768)
+
+        def spread_came(o, carry):
+            source = lax.rem(k + o, STEPS)
+            block = plane_block(source)
+            remote(
+                block, block, plane_send.at[o], plane_recv.at[source], {"step": source}
+            ).wait_recv()
+            return carry
+
+        lax.fori_loop(1, STEPS, spread_came, 0)
+        for h in range(2):
+            plane_across(c, h).start()
+        onward(0, 2, 1, 2)
+        for h in range(2):
+            plane_across(other, h).wait_recv()
+        project(0, 768, both(3) + both(4) + both(5))
+        older(768, 1536)
+        newer(768, 1536)
+        other_half_came(0, -2)
+        other_half_came(0, 2)
+        project(0, 1536, both(rel(-2)) + both(rel(2)))
+        finish(0, 1536, (4, 3, 5, 1, 2, 6, 7, 0))
+
+    def gather_second():
+        other_half_came(1, 0)
+        project(1, 0, both(0))
+        newer(0, TILE)
+        onward(1, 1, 0, 4)
         for i in range(1, 5):
-            behind = lax.rem(z - i * sign + RING, RING)
-            ahead = lax.rem(z + i * sign + RING, RING)
-            ring(t, slot(behind, c), maj_send.at[t, 0], z_major).wait_recv()
+            onward(1, i, 1, 4)
+            other_half_came(1, -i)
+            slots = both(rel(-i))
             if i < 4:
-                ring(t, slot(behind, c), maj_send.at[t, i], z_major).start()
-            across(t, slot(behind, c), i).start()
-            if i < 4:
-                ring(t, slot(ahead, c), min_send.at[t, 0], z_minor).wait_recv()
-                if i < 3:
-                    ring(t, slot(ahead, c), min_send.at[t, i], z_minor).start()
-                across(t, slot(ahead, c), 4 + i).start()
-            across(t, slot(behind, other), 0).wait_recv()
-            slots = [slot(behind, c), slot(behind, other)]
-            if i < 4:
-                across(t, slot(ahead, other), 0).wait_recv()
-                slots += [slot(ahead, c), slot(ahead, other)]
+                other_half_came(1, i)
+                slots = slots + both(rel(i))
             low = TILE + 2 * TILE * (i - 1)
             high = low + len(slots) * CHUNK
-            project(t, low, slots)
+            project(1, low, slots)
             if i < 4:
                 older(low, high)
+                onward(1, i + 1, 0, 4)
                 newer(low, high)
-        last = FRAMES - TILE
-        for i in (5, 6, 3, 4, 1, 2, 7, 0):
-            if i == 7:
-                total = attend(last, 0, FRAMES, zero)
+        finish(1, FRAMES - TILE, (5, 6, 3, 4, 1, 2, 7, 0))
+
+    def finish(t, last, order):
+        for i in order:
+            if i * TILE >= last:
+                total = attend(i * TILE, 0, FRAMES, zero)
             else:
                 total = attend(i * TILE, last, FRAMES, acc[i * TILE : (i + 1) * TILE, :])
             result = (total[:, :128] / total[:, 128:]).astype(BF16)
@@ -382,7 +511,7 @@
     def increment(j):
         return jnp.concatenate([incs[j]] * (WIDTH // 128), axis=1)
 
-    gather_and_attend(0)
+    gather_first()
     loads[3].wait()
     gate_copy_back = remote(
         gates.at[other], gates.at[other], pair_send.at[0], pair_recv.at[0], {"cfg": other}
@@ -410,10 +539,10 @@
         total = total + (increment(j) * start_rows + terms[j])
     nb[0] = fold(layer_norm(states[...]))
     exchange(nb, nr, n_send, n_recv, 0)
-    xall[1, mine] = unfold(nr[0]).reshape(CHUNK, WIDTH).astype(BF16)
+    xall[1, 0, c] = unfold(nr[0]).reshape(CHUNK, WIDTH).astype(BF16)
 
     begin(1)
-    gather_and_attend(1)
+    gather_second()
     terms = merge(1)
     total = jnp.zeros_like(start_rows)
     drifts = []
@@ -440,16 +569,30 @@
         return carry
 
     lax.fori_loop(1, STEPS, inc_left, 0)
+    for i in range(3):
+        far_copy(i).wait_send()
+    for h in range(2):
+        plane_across(c, h).wait_send()
+
+    def plane_left(o, carry):
+        plane_copy(o).wait_send()
+        return carry
+
+    lax.fori_loop(1, STEPS, plane_left, 0)
     for t in range(2):
         for i in range(8):
-            across(t, mine, i).wait_send()
             for side in range(2):
                 if i or side:
                     result_copy(t, i, side).wait_send()
-        for i in range(4):
-            ring(t, mine, maj_send.at[t, i], z_major).wait_send()
-        for i in range(3):
-            ring(t, mine, min_send.at[t, i], z_minor).wait_send()
+        hops = (2, 4)[t]
+        for h in range(2):
+            across(t, 0, h, c).wait_send()
+            for i in range(hops):
+                major(t, i, h).wait_send()
+                across(t, -(i + 1), h, c).wait_send()
+            for i in range(min(hops, 3)):
+                minor(t, i, h).wait_send()
+                across(t, i + 1, h, c).wait_send()
 
 
 def local(clip, ordinal, strength, increment, table, pair, w_in, w_merge, sharp):
@@ -463,7 +606,7 @@
         in_specs=[vmem, smem, smem, smem, vmem, vmem, anywhere, anywhere, smem],
         out_specs=vmem,
         scratch_shapes=[
-            pltpu.VMEM((2, COLUMN, CHUNK, WIDTH), BF16),
+            pltpu.VMEM((2, RING, 2, CHUNK, WIDTH), BF16),
             pltpu.VMEM((3, WIDTH, 128), BF16),
             pltpu.VMEM((WIDTH, 384), BF16),
             pltpu.VMEM((WIDTH, WIDTH), BF16),
@@ -483,10 +626,14 @@
             pltpu.VMEM((2, 8, WIDTH), F32),
             pltpu.VMEM((STEPS, 8, 128), F32),
             dma((4,)),
-            dma((2, 4)),
-            dma((2, 3)),
-            dma((2, 8)),
-            dma((2, COLUMN)),
+            dma((2, 4, 2)),
+            dma((2, 3, 2)),
+            dma((2, RING, 2)),
+            dma((2, RING, 2, 2)),
+            dma((5,)),
+            dma((5,)),
+            dma((STEPS,)),
+            dma((STEPS,)),
             dma((2, COLUMN)),
             dma((2, COLUMN)),
             dma((2, STEPS)),

time: 139 us -> 136 us (0.978)
  Pallas kernels: 135 us -> 132 us
    pallas_call x1, Pallas kernels: 135 us -> 132 us  [local(): pl.pallas_call(kernel, out_shape=jax.ShapeDtypeStruct(clip.shape, F32), i...]
where the time goes in v2:
time: 136 us
  Pallas kernels  132 us (97%)
  local copies, waits for them, and re-layouts  2.31 us (2%)
  between operations  1.95 us (1%)
    pallas_call x1, Pallas kernels, local(): pl.pallas_call(kernel, out_shape=jax.ShapeDtypeStruct(clip.shape, F32), i...  132 us

profile of v2, /device:TPU:1, one launch (start us, length us, event | category | flops | bytes accessed | tf_op | source)
XLA Modules:
  0.0 135.9 jit_solution(9414178100832871401)
XLA Ops:
  1.9 131.6 %shard_map.91 = f32[256,1024]{1,0:T(8,128)} custom-call(f32[256,1024]{1,0:T(8,128)} %clip_ref.1, s32[1]{0:T(128)S(6)} %copy.11.ordinal_ref, f32[1]{0:T(128)S(6)} %copy.12.strength_ref, f32[1]{0:T(128)S(6)} %copy.13.increment_ref, bf16[50,3072]{1,0:T(8,128)(2,1)} %table_ref.1, bf16[1,3072]{1,0:T(2,128)(2,1)} %pair_ref.1, bf16[1024,3072]{1,0:T(8,128)(2,1)} %w_in_ref.1, ...), custom_call_target="tpu_custom_call" | custom-call | tf_op jit(solution)/shard_map/pallas_call | solution.py:603
  133.6 2.3 %copy.14 = f32[1,256,1024]{2,1,0:T(8,128)} copy(f32[1,256,1024]{2,1,0:T(8,128)} %bitcast.1) | data formatting | bytes 2097152

commit v3 on v2

v3 whole, which is shorter than its diff:
```python
import math

import jax
import jax.numpy as jnp
from jax import lax
from jax.experimental import pallas as pl
from jax.experimental.pallas import tpu as pltpu
from jax.sharding import PartitionSpec as P

MESH = pl.DeviceIdType.MESH
F32 = jnp.float32
BF16 = jnp.bfloat16
LOG2E = 1.4426950408889634

WIDTH = 1024
FRAMES = 2048
HALF = 64
CHUNK = 128
TILE = 256
RING = 8
STEPS = 16
COLUMN = 16


def remote(src, dst, send_sem, recv_sem, device):
    return pltpu.make_async_remote_copy(
        src_ref=src,
        dst_ref=dst,
        send_sem=send_sem,
        recv_sem=recv_sem,
        device_id=device,
        device_id_type=MESH,
    )


def fold(rows):
    half = WIDTH // 2
    return jnp.concatenate([rows[:, :, :half], rows[:, :, half:]], axis=1).astype(BF16)


def unfold(tiles):
    wide = tiles.astype(F32)
    return jnp.concatenate([wide[:, :8], wide[:, 8:]], axis=2)


def layer_norm(rows):
    average = jnp.mean(rows, axis=-1, keepdims=True)
    centred = rows - average
    variance = jnp.mean(centred * centred, axis=-1, keepdims=True)
    return centred * lax.rsqrt(variance + 1e-06)


def kernel(
    clip_ref,
    ordinal_ref,
    strength_ref,
    increment_ref,
    table_ref,
    pair_ref,
    w_in_ref,
    w_merge_ref,
    sharp_ref,
    out_ref,
    xall,
    w_raw,
    w_mod,
    w_out,
    bias,
    qb,
    kb,
    vt,
    acc,
    ob,
    att,
    sb,
    rb,
    nb,
    nr,
    fin,
    states,
    gates,
    incs,
    out_rows,
    local_sem,
    maj_send,
    min_send,
    d2d_send,
    ring_recv,
    far_send,
    far_recv,
    plane_send,
    plane_recv,
    a2a_send,
    a2a_recv,
    s_send,
    s_recv,
    n_send,
    n_recv,
    inc_send,
    inc_recv,
    pair_send,
    pair_recv,
):
    k = lax.axis_index("step")
    c = lax.axis_index("cfg")
    z = lax.axis_index("seq")
    other = 1 - c
    sign = 1 - 2 * c
    mine = 2 * z + c

    barrier = pltpu.get_barrier_semaphore()

    def greet(o, carry):
        e = lax.rem(mine + o, COLUMN)
        pl.semaphore_signal(
            barrier, inc=1, device_id={"seq": e // 2, "cfg": lax.rem(e, 2)}, device_id_type=MESH
        )
        pl.semaphore_signal(
            barrier, inc=1, device_id={"step": lax.rem(k + o, STEPS)}, device_id_type=MESH
        )
        return carry

    lax.fori_loop(1, COLUMN, greet, 0)

    loads = []
    for part in range(3):
        columns = pl.ds(pl.multiple_of(part * WIDTH + z * 128, 128), 128)
        loads.append(
            pltpu.make_async_copy(
                w_in_ref.at[:, columns], w_raw.at[part], local_sem.at[part]
            )
        )
    loads.append(pltpu.make_async_copy(w_merge_ref, w_out, local_sem.at[3]))
    for load in loads:
        load.start()

    own_rows = pl.ds(pl.multiple_of(c * CHUNK, CHUNK), CHUNK)
    xall[0, 0, c] = layer_norm(clip_ref[own_rows, :]).astype(BF16)

    lane = lax.broadcasted_iota(jnp.int32, (1, 128), 1)
    first_head = lane < 64

    chosen = (
        lax.broadcasted_iota(jnp.int32, (16, table_ref.shape[0]), 1) == ordinal_ref[0]
    ).astype(BF16)
    affine = jnp.dot(chosen, table_ref[...], preferred_element_type=F32)[:8] + pair_ref[
        ...
    ].astype(F32)
    shift = affine[:, :WIDTH]
    scale_now = strength_ref[0]
    step_now = increment_ref[0]
    share = jnp.where(c == 0, scale_now, 1.0 - scale_now) * step_now
    gates[c] = affine[:, 2 * WIDTH :] * share
    incs[k] = jnp.full((8, 128), step_now, F32)
    scale_column = jnp.transpose(
        jnp.broadcast_to(1.0 + affine[:1, WIDTH : 2 * WIDTH], (128, WIDTH))
    )
    shift_high = shift.astype(BF16)
    shift_low = shift - shift_high.astype(F32)
    shift_parts = jnp.concatenate([shift_high.astype(F32), shift_low], axis=0).astype(BF16)
    for part in range(3):
        loads[part].wait()
        raw = w_raw[part]
        both = jnp.dot(shift_parts, raw, preferred_element_type=F32)
        bias[:, part * 128 : (part + 1) * 128] = both[:8] + both[8:]
        w_mod[:, part * 128 : (part + 1) * 128] = (raw.astype(F32) * scale_column).astype(BF16)
    for h in range(2):
        vt[h, 64:, :] = jnp.ones((16, FRAMES), BF16)
    q_scale = jnp.where(first_head, sharp_ref[2 * z], sharp_ref[2 * z + 1]) * (
        LOG2E / math.sqrt(64.0)
    )
    same_head = (
        (lax.broadcasted_iota(jnp.int32, (128, 128), 0) < 64)
        == (lax.broadcasted_iota(jnp.int32, (128, 128), 1) < 64)
    ).astype(F32).astype(BF16)

    pl.semaphore_wait(barrier, 2 * (COLUMN - 1))

    def rel(offset):
        return lax.rem(offset * sign + RING, RING)

    def half_rows(h):
        return pl.ds(h * HALF, HALF)

    def at(t, offset, core, h):
        return xall.at[t, rel(offset), core, half_rows(h)]

    z_major = lax.rem(z + sign + RING, RING)
    z_minor = lax.rem(z - sign + RING, RING)

    def major(t, i, h):
        return remote(
            at(t, -i, c, h),
            at(t, -(i + 1), c, h),
            maj_send.at[t, i, h],
            ring_recv.at[t, rel(-(i + 1)), c, h],
            {"seq": z_major},
        )

    def minor(t, i, h):
        return remote(
            at(t, i, c, h),
            at(t, i + 1, c, h),
            min_send.at[t, i, h],
            ring_recv.at[t, rel(i + 1), c, h],
            {"seq": z_minor},
        )

    def across(t, offset, h, core):
        block = at(t, offset, core, h)
        return remote(
            block,
            block,
            d2d_send.at[t, rel(offset), h],
            ring_recv.at[t, rel(offset), core, h],
            {"cfg": other},
        )

    def begin(t, h):
        major(t, 0, h).start()
        minor(t, 0, h).start()
        across(t, 0, h, c).start()

    def onward(t, i, h, hops):
        major(t, i - 1, h).wait_recv()
        if i < hops:
            major(t, i, h).start()
        across(t, -i, h, c).start()
        if i < 4:
            minor(t, i - 1, h).wait_recv()
            if i < min(hops, 3):
                minor(t, i, h).start()
            across(t, i, h, c).start()

    def other_half_came(t, offset):
        for h in range(2):
            across(t, offset, h, other).wait_recv()

    x, y = lax.rem(k, 4), k // 4
    one, two = x + c * (y - x), y + c * (x - y)
    step_one, step_two = 1 + 3 * c, 4 - 3 * c

    def piece_rows(index):
        return pl.ds(pl.multiple_of(index * 32, 32), 32)

    def piece_lanes(index):
        return pl.ds(pl.multiple_of(index * 256, 256), 256)

    def far_copy(i):
        return remote(
            xall.at[0, 0, c, piece_rows(two), piece_lanes(one)],
            xall.at[0, 3 + i, c, piece_rows(two), piece_lanes(one)],
            far_send.at[i],
            far_recv.at[i],
            {"seq": lax.rem(z + 5 - i, RING)},
        )

    def plane_one(o, came=False):
        peer = lax.rem(one + o, 4)
        block = xall.at[
            0, pl.ds(3, 3), c, piece_rows(two), piece_lanes(peer if came else one)
        ]
        return remote(
            block,
            block,
            plane_send.at[0, o],
            plane_recv.at[0, peer if came else one],
            {"step": k + (peer - one) * step_one},
        )

    def plane_two(o, came=False):
        peer = lax.rem(two + o, 4)
        block = xall.at[0, pl.ds(3, 3), c, piece_rows(peer if came else two)]
        return remote(
            block,
            block,
            plane_send.at[1, o],
            plane_recv.at[1, peer if came else two],
            {"step": k + (peer - two) * step_two},
        )

    def plane_half(core, h):
        return xall.at[0, pl.ds(3, 3), core, half_rows(h)]

    def plane_across(core, h):
        block = plane_half(core, h)
        return remote(block, block, far_send.at[3 + h], far_recv.at[3 + h], {"cfg": other})

    for i in range(3):
        far_copy(i).start()
    for h in range(2):
        begin(0, h)
    gate_copy = remote(
        gates.at[c], gates.at[c], pair_send.at[0], pair_recv.at[0], {"cfg": other}
    )
    gate_copy.start()

    def inc_copy(o):
        return remote(
            incs.at[k],
            incs.at[k],
            inc_send.at[o],
            inc_recv.at[k],
            {"step": lax.rem(k + o, STEPS)},
        )

    def send_inc(o, carry):
        inc_copy(o).start()
        return carry

    def project(t, start, slots):
        rows = len(slots) * CHUNK
        block = jnp.concatenate([xall[t, slab, core] for slab, core in slots], axis=0)
        qkv = jnp.dot(block, w_mod[...], preferred_element_type=F32) + bias[:1, :]
        here = pl.ds(start, rows)

        def normalize(values):
            squares = jnp.dot(
                (values * values).astype(BF16), same_head, preferred_element_type=F32
            )
            return values * lax.rsqrt(squares * (1.0 / 64.0) + 1e-06)

        queries = normalize(qkv[:, :128]) * q_scale
        for i in range(0, rows, TILE):
            parts = [queries[i + r : i + r + HALF] for r in (0, CHUNK, HALF, CHUNK + HALF)]
            qb[pl.ds(start + i, TILE), :] = jnp.concatenate(parts, axis=0).astype(BF16)
        keys = normalize(qkv[:, 128:256])
        values = jnp.transpose(qkv[:, 256:])
        for h in range(2):
            mask = first_head if h == 0 else jnp.logical_not(first_head)
            kb[h, here, :] = jnp.where(mask, keys, 0.0).astype(BF16)
            vt[h, :64, here] = values[h * 64 : (h + 1) * 64].astype(BF16)

    def attend(q, low, high, totals):
        totals = list(totals)
        for j in range(low, high, 1024):
            end = min(j + 1024, high)
            for h in range(2):
                scores = lax.dot_general(
                    kb[h, j:end, :], q, (((1,), (1,)), ((), ())), preferred_element_type=F32
                )
                powers = jnp.exp2(scores).astype(BF16)
                totals[h] = totals[h] + jnp.dot(
                    vt[h, :, j:end], powers, preferred_element_type=F32
                )
        return totals

    def zeros(count):
        return [jnp.zeros((80, count), F32)] * 2

    def pieces(low, high):
        count = -(-(high - low) // 1024)
        each = (high - low) // count
        return [(low + n * each, low + (n + 1) * each) for n in range(count)]

    def older(low, high):
        for a, b in pieces(0, low):
            totals = attend(qb[a:b, :], low, high, [acc[0, :, a:b], acc[1, :, a:b]])
            for h in range(2):
                acc[h, :, a:b] = totals[h]

    def newer(low, high, last):
        for a, b in pieces(low, high):
            totals = attend(qb[a:b, :], 0, last, zeros(b - a))
            for h in range(2):
                acc[h, :, a:b] = totals[h]

    def place(t, i):
        if t == 0 and i > 4:
            return i - 2
        return rel(-(i + 1) // 2 if i % 2 else i // 2)

    def result_copy(t, h, i, side):
        target = {"seq": lax.rem(z + place(t, i), RING), "cfg": c if side == 0 else other}
        return remote(
            ob.at[t, h, 2 * i + side],
            att.at[t, h, c, z],
            a2a_send.at[t, h, 2 * i + side],
            a2a_recv.at[t, h, mine],
            target,
        )

    def both(slab):
        return [(slab, c), (slab, other)]

    def gather_first():
        other_half_came(0, 0)
        project(0, 0, both(0))
        newer(0, TILE, TILE)
        for i in range(3):
            far_copy(i).wait_recv()
        for o in (2, 1, 3):
            plane_one(o).start()
        lax.fori_loop(1, STEPS, send_inc, 0)
        onward(0, 1, 0, 2)
        onward(0, 1, 1, 2)
        other_half_came(0, -1)
        other_half_came(0, 1)
        project(0, 256, both(rel(-1)) + both(rel(1)))
        older(256, 768)
        for o in (1, 3, 2):
            plane_one(o, came=True).wait_recv()
        for o in (2, 1, 3):
            plane_two(o).start()
        newer(256, 768, 768)
        onward(0, 2, 0, 2)
        onward(0, 2, 1, 2)
        other_half_came(0, -2)
        other_half_came(0, 2)
        project(0, 768, both(rel(-2)) + both(rel(2)))
        older(768, 1280)
        for o in (1, 3, 2):
            plane_two(o, came=True).wait_recv()
        for h in range(2):
            plane_across(c, h).start()
        newer(768, 1280, 1280)
        for h in range(2):
            plane_across(other, h).wait_recv()
        project(0, 1280, both(3) + both(4) + both(5))
        finish(0, 1280, (6, 5, 7, 3, 4, 1, 2, 0))

    def gather_second():
        other_half_came(1, 0)
        project(1, 0, both(0))
        newer(0, TILE, TILE)
        onward(1, 2, 0, 4)
        for i in range(1, 5):
            onward(1, i, 1, 4)
            other_half_came(1, -i)
            slots = both(rel(-i))
            if i < 4:
                other_half_came(1, i)
                slots = slots + both(rel(i))
            low = TILE + 2 * TILE * (i - 1)
            high = low + len(slots) * CHUNK
            project(1, low, slots)
            if i < 4:
                older(low, high)
                if i < 3:
                    onward(1, i + 2, 0, 4)
                newer(low, high, high)
        finish(1, FRAMES - TILE, (7, 5, 6, 3, 4, 1, 2, 0))

    def each_result(t, h, order, act):
        for i in order:
            for side in range(2):
                if i or side:
                    act(result_copy(t, h, i, side))

    def finish(t, last, order):
        newer(last, FRAMES, last)
        for half in range(2):
            starts = [i * TILE + half * CHUNK for i in order]
            totals = attend(
                jnp.concatenate([qb[r : r + CHUNK, :] for r in starts], axis=0),
                last,
                FRAMES,
                [
                    jnp.concatenate([acc[h, :, r : r + CHUNK] for r in starts], axis=1)
                    for h in range(2)
                ],
            )
            result = jnp.transpose(
                jnp.concatenate([a[:64] * (1.0 / a[64:65]) for a in totals], axis=0)
            ).astype(BF16)
            for n, i in enumerate(order):
                for side in range(2):
                    start = n * CHUNK + side * HALF
                    piece = result[start : start + HALF]
                    if i == 0 and side == 0:
                        att[t, half, c, z] = piece
                    else:
                        ob[t, half, 2 * i + side] = piece
            each_result(t, half, order, lambda copy: copy.start())

    colour = lax.rem(x + y, 2)

    def owner(spot, h):
        return 2 * spot + lax.rem(spot // 2 + h, 2)

    def clip_rows():
        start = c * CHUNK + colour * HALF + k // 2 * 8
        return clip_ref[pl.ds(pl.multiple_of(start, 8), 8), :]

    def term_copy(t, h, j):
        spot = lax.rem(j + k // 2, 8)
        return remote(
            sb.at[t, h, spot],
            rb.at[t, k],
            s_send.at[t, h, spot],
            s_recv.at[t, k],
            {"step": owner(spot, h)},
        )

    def each_owner(t, h, act):
        def one_owner(j, carry):
            @pl.when(owner(lax.rem(j + k // 2, 8), h) != k)
            def _():
                act(term_copy(t, h, j))

            return carry

        lax.fori_loop(0, 8, one_owner, 0)

    def back_copy(t, o):
        target = lax.rem(k + o, STEPS)
        return remote(
            nb.at[t, target],
            nr.at[t, colour, k // 2],
            n_send.at[t, o],
            n_recv.at[t, k],
            {"step": target},
        )

    def merge(t, h):
        def arrive(o, carry):
            e = lax.rem(mine + o, COLUMN)
            zz, cc = e // 2, lax.rem(e, 2)
            remote(
                ob.at[t, h, 0],
                att.at[t, h, cc, zz],
                a2a_send.at[t, h, 0],
                a2a_recv.at[t, h, e],
                {"seq": zz, "cfg": cc},
            ).wait_recv()
            return carry

        lax.fori_loop(1, COLUMN, arrive, 0)
        attended = jnp.concatenate(
            [
                jnp.concatenate([att[t, h, cc, zz] for zz in range(RING)], axis=1)
                for cc in range(2)
            ],
            axis=0,
        )
        projected = jnp.dot(attended, w_out[...], preferred_element_type=F32)
        terms = projected[:HALF] * gates[0, :1, :] + projected[HALF:] * gates[1, :1, :]
        sb[t, h] = fold(terms.reshape(8, 8, WIDTH))

    def send_terms(t, h):
        each_owner(t, h, lambda copy: copy.start())

    def own(t, h):
        @pl.when(colour == h)
        def _():
            rb[t, k] = sb[t, h, k // 2]

            def arrive(o, carry):
                source = lax.rem(k + o, STEPS)
                remote(
                    sb.at[t, 0, 0],
                    rb.at[t, source],
                    s_send.at[t, 0, 0],
                    s_recv.at[t, source],
                    {"step": source},
                ).wait_recv()
                return carry

            lax.fori_loop(1, STEPS, arrive, 0)
            terms = unfold(rb[t])
            start_rows = clip_rows()
            total = jnp.zeros_like(start_rows)
            if t == 0:
                for j in range(STEPS):
                    states[j] = start_rows + total
                    total = total + (increment(j) * start_rows + terms[j])
                nb[0] = fold(layer_norm(states[...]))
            else:
                drifts = []
                for j in range(STEPS):
                    total = total + (increment(j) * states[j] + terms[j])
                    drifts.append(total)
                nb[1] = fold(jnp.stack(drifts, axis=0))

            def back(o, carry):
                back_copy(t, o).start()
                return carry

            lax.fori_loop(1, STEPS, back, 0)
            nr[t, h, k // 2] = nb[t, k]

    def rows_back(t, h):
        def arrive(j, carry):
            source = owner(lax.rem(j + k // 2, 8), h)

            @pl.when(source != k)
            def _():
                remote(
                    nb.at[t, 0],
                    nr.at[t, h, source // 2],
                    n_send.at[t, 0],
                    n_recv.at[t, source],
                    {"step": source},
                ).wait_recv()

            return carry

        lax.fori_loop(0, 8, arrive, 0)
        return unfold(nr[t, h]).reshape(HALF, WIDTH)

    def next_rows(h):
        xall[1, 0, c, half_rows(h)] = rows_back(0, h).astype(BF16)
        begin(1, h)

    def final_copy(h):
        return remote(
            nr.at[1, h], fin.at[h], pair_send.at[1 + h], pair_recv.at[1 + h], {"cfg": other}
        )

    def out_copy(rows, i):
        return pltpu.make_async_copy(
            out_rows.at[rows], out_ref.at[rows], local_sem.at[4 + i]
        )

    def own_out(h):
        rows = pl.ds(pl.multiple_of(c * CHUNK + h * HALF, HALF), HALF)
        drift = rows_back(1, h)
        final_copy(h).start()
        out_rows[rows, :] = clip_ref[rows, :] + drift
        out_copy(rows, h).start()

    def increment(j):
        return jnp.concatenate([incs[j]] * (WIDTH // 128), axis=1)

    def ring_left(t):
        hops = (2, 4)[t]
        for h in range(2):
            across(t, 0, h, c).wait_send()
            for i in range(hops):
                major(t, i, h).wait_send()
                across(t, -(i + 1), h, c).wait_send()
            for i in range(min(hops, 3)):
                minor(t, i, h).wait_send()
                across(t, i + 1, h, c).wait_send()

    def exchange_left(t):
        def left(o, carry):
            back_copy(t, o).wait_send()
            return carry

        lax.fori_loop(1, STEPS, left, 0)
        for h in range(2):
            each_owner(t, h, lambda copy: copy.wait_send())

    def inc_left(o, carry):
        inc_copy(o).wait_send()
        return carry

    gather_first()
    loads[3].wait()
    gate_copy_back = remote(
        gates.at[other], gates.at[other], pair_send.at[0], pair_recv.at[0], {"cfg": other}
    )
    gate_copy_back.wait_recv()

    def inc_arrive(o, carry):
        source = lax.rem(k + o, STEPS)
        remote(
            incs.at[source],
            incs.at[source],
            inc_send.at[o],
            inc_recv.at[source],
            {"step": source},
        ).wait_recv()
        return carry

    lax.fori_loop(1, STEPS, inc_arrive, 0)

    merge(0, 0)
    send_terms(0, 0)
    own(0, 0)
    merge(0, 1)
    send_terms(0, 1)
    next_rows(0)
    own(0, 1)
    onward(1, 1, 0, 4)
    next_rows(1)

    gate_copy.wait_send()
    ring_left(0)
    exchange_left(0)
    for h in range(2):
        each_result(0, h, range(8), lambda copy: copy.wait_send())
    lax.fori_loop(1, STEPS, inc_left, 0)
    for i in range(3):
        far_copy(i).wait_send()
    for h in range(2):
        plane_across(c, h).wait_send()
    for o in range(1, 4):
        plane_one(o).wait_send()
        plane_two(o).wait_send()

    gather_second()
    ring_left(1)
    merge(1, 0)
    merge(1, 1)
    send_terms(1, 0)
    send_terms(1, 1)
    for h in range(2):
        each_result(1, h, range(8), lambda copy: copy.wait_send())
    for h in range(2):
        own(1, h)
    own_out(0)
    own_out(1)
    for h in range(2):
        rows = pl.ds(pl.multiple_of(other * CHUNK + h * HALF, HALF), HALF)
        final_copy(h).wait_recv()
        out_rows[rows, :] = clip_ref[rows, :] + unfold(fin[h]).reshape(HALF, WIDTH)
        out_copy(rows, 2 + h).start()
    exchange_left(1)
    for h in range(2):
        final_copy(h).wait_send()
        out_copy(half_rows(h), h).wait()
        out_copy(half_rows(h), 2 + h).wait()


def local(clip, ordinal, strength, increment, table, pair, w_in, w_merge, sharp):
    vmem = pl.BlockSpec(memory_space=pltpu.VMEM)
    smem = pl.BlockSpec(memory_space=pltpu.SMEM)
    anywhere = pl.BlockSpec(memory_space=pl.ANY)
    dma = pltpu.SemaphoreType.DMA
    out = pl.pallas_call(
        kernel,
        out_shape=jax.ShapeDtypeStruct(clip.shape, F32),
        in_specs=[vmem, smem, smem, smem, vmem, vmem, anywhere, anywhere, smem],
        out_specs=anywhere,
        scratch_shapes=[
            pltpu.VMEM((2, RING, 2, CHUNK, WIDTH), BF16),
            pltpu.VMEM((3, WIDTH, 128), BF16),
            pltpu.VMEM((WIDTH, 384), BF16),
            pltpu.VMEM((WIDTH, WIDTH), BF16),
            pltpu.VMEM((8, 384), F32),
            pltpu.VMEM((FRAMES, 128), BF16),
            pltpu.VMEM((2, FRAMES, 128), BF16),
            pltpu.VMEM((2, 80, FRAMES), BF16),
            pltpu.VMEM((2, 80, FRAMES), F32),
            pltpu.VMEM((2, 2, COLUMN, HALF, 128), BF16),
            pltpu.VMEM((2, 2, 2, RING, HALF, 128), BF16),
            pltpu.VMEM((2, 2, 8, 16, 512), BF16),
            pltpu.VMEM((2, STEPS, 16, 512), BF16),
            pltpu.VMEM((2, STEPS, 16, 512), BF16),
            pltpu.VMEM((2, 2, 8, 16, 512), BF16),
            pltpu.VMEM((2, 8, 16, 512), BF16),
            pltpu.VMEM((STEPS, 8, WIDTH), F32),
            pltpu.VMEM((2, 8, WIDTH), F32),
            pltpu.VMEM((STEPS, 8, 128), F32),
            pltpu.VMEM((2 * CHUNK, WIDTH), F32),
            dma((8,)),
            dma((2, 4, 2)),
            dma((2, 3, 2)),
            dma((2, RING, 2)),
            dma((2, RING, 2, 2)),
            dma((5,)),
            dma((5,)),
            dma((2, 4)),
            dma((2, 4)),
            dma((2, 2, COLUMN)),
            dma((2, 2, COLUMN)),
            dma((2, 2, 8)),
            dma((2, STEPS)),
            dma((2, STEPS)),
            dma((2, STEPS)),
            dma((STEPS,)),
            dma((STEPS,)),
            dma((3,)),
            dma((3,)),
        ],
        compiler_params=pltpu.CompilerParams(
            collective_id=0, has_side_effects=True, vmem_limit_bytes=56 * 2**20
        ),
    )(clip, ordinal, strength, increment, table, pair, w_in, w_merge, sharp)
    return out[None]


def solution(mesh):
    placed = (P("seq", None), P("step"), P("step"), P("step"), P(), P("cfg", None), P(), P(), P())
    return jax.shard_map(
        local, mesh=mesh, in_specs=placed, out_specs=P("step", "seq", None), check_vma=False
    )
```

time: 136 us -> 127 us (0.934)
  Pallas kernels: 132 us -> 122 us
    pallas_call x1, Pallas kernels: 132 us -> 122 us  [local(): pl.pallas_call(kernel, out_shape=jax.ShapeDtypeStruct(clip.shape, F32), i...]
where the time goes in v3:
time: 127 us; the launch traced here: 126 us
  Pallas kernels  122 us (96%)
  local copies, waits for them, and re-layouts  2.31 us (2%)
  between operations  1.95 us (2%)
    pallas_call x1, Pallas kernels, local(): pl.pallas_call(kernel, out_shape=jax.ShapeDtypeStruct(clip.shape, F32), i...  122 us

profile of v3, /device:TPU:1, one launch (start us, length us, event | category | flops | bytes accessed | tf_op | source)
XLA Modules:
  0.0 126.4 jit_solution(7211800830485604536)
XLA Ops:
  1.9 122.2 %shard_map.91 = f32[256,1024]{1,0:T(8,128)} custom-call(f32[256,1024]{1,0:T(8,128)} %clip_ref.1, s32[1]{0:T(128)S(6)} %copy.11.ordinal_ref, f32[1]{0:T(128)S(6)} %copy.12.strength_ref, f32[1]{0:T(128)S(6)} %copy.13.increment_ref, bf16[50,3072]{1,0:T(8,128)(2,1)} %table_ref.1, bf16[1,3072]{1,0:T(2,128)(2,1)} %pair_ref.1, bf16[1024,3072]{1,0:T(8,128)(2,1)} %w_in_ref.1, ...), custom_call_target="tpu_custom_call" | custom-call | tf_op jit(solution)/shard_map/pallas_call | solution.py:722
  124.1 2.3 %copy.14 = f32[1,256,1024]{2,1,0:T(8,128)} copy(f32[1,256,1024]{2,1,0:T(8,128)} %bitcast.1) | data formatting | bytes 2097152

commit v4 on v3

--- a/solution.py
+++ b/solution.py
@@ -176,6 +176,12 @@
 
     pl.semaphore_wait(barrier, 2 * (COLUMN - 1))
 
+    def left_all(block, send_sem):
+        remote(block, block, send_sem, pair_recv.at[0], {"cfg": other}).wait_send()
+
+    def came_all(block, recv_sem):
+        remote(block, block, pair_send.at[0], recv_sem, {"cfg": other}).wait_recv()
+
     def rel(offset):
         return lax.rem(offset * sign + RING, RING)
 
@@ -192,7 +198,7 @@
         return remote(
             at(t, -i, c, h),
             at(t, -(i + 1), c, h),
-            maj_send.at[t, i, h],
+            maj_send.at[t],
             ring_recv.at[t, rel(-(i + 1)), c, h],
             {"seq": z_major},
         )
@@ -201,7 +207,7 @@
         return remote(
             at(t, i, c, h),
             at(t, i + 1, c, h),
-            min_send.at[t, i, h],
+            min_send.at[t],
             ring_recv.at[t, rel(i + 1), c, h],
             {"seq": z_minor},
         )
@@ -211,7 +217,7 @@
         return remote(
             block,
             block,
-            d2d_send.at[t, rel(offset), h],
+            d2d_send.at[t],
             ring_recv.at[t, rel(offset), core, h],
             {"cfg": other},
         )
@@ -250,41 +256,40 @@
         return remote(
             xall.at[0, 0, c, piece_rows(two), piece_lanes(one)],
             xall.at[0, 3 + i, c, piece_rows(two), piece_lanes(one)],
-            far_send.at[i],
-            far_recv.at[i],
+            far_send.at[0],
+            far_recv.at[0],
             {"seq": lax.rem(z + 5 - i, RING)},
         )
 
-    def plane_one(o, came=False):
+    def plane_one(o):
         peer = lax.rem(one + o, 4)
-        block = xall.at[
-            0, pl.ds(3, 3), c, piece_rows(two), piece_lanes(peer if came else one)
-        ]
+        block = xall.at[0, pl.ds(3, 3), c, piece_rows(two), piece_lanes(one)]
         return remote(
             block,
             block,
-            plane_send.at[0, o],
-            plane_recv.at[0, peer if came else one],
+            plane_send.at[0],
+            plane_recv.at[0],
             {"step": k + (peer - one) * step_one},
         )
 
-    def plane_two(o, came=False):
+    def plane_two(o):
         peer = lax.rem(two + o, 4)
-        block = xall.at[0, pl.ds(3, 3), c, piece_rows(peer if came else two)]
+        block = xall.at[0, pl.ds(3, 3), c, piece_rows(two)]
         return remote(
             block,
             block,
-            plane_send.at[1, o],
-            plane_recv.at[1, peer if came else two],
+            plane_send.at[1],
+            plane_recv.at[1],
             {"step": k + (peer - two) * step_two},
         )
 
-    def plane_half(core, h):
-        return xall.at[0, pl.ds(3, 3), core, half_rows(h)]
-
-    def plane_across(core, h):
-        block = plane_half(core, h)
-        return remote(block, block, far_send.at[3 + h], far_recv.at[3 + h], {"cfg": other})
+    def plane_across(core):
+        block = xall.at[0, pl.ds(3, 3), core]
+        return remote(block, block, far_send.at[1], far_recv.at[1], {"cfg": other})
+
+    far_bytes = xall.at[0, pl.ds(0, 3), 0, pl.ds(0, 32), pl.ds(0, 256)]
+    one_bytes = xall.at[0, pl.ds(0, 3), 0, pl.ds(0, 32), pl.ds(0, 768)]
+    two_bytes = xall.at[0, pl.ds(0, 3), 0, pl.ds(0, 96)]
 
     for i in range(3):
         far_copy(i).start()
@@ -299,8 +304,8 @@
         return remote(
             incs.at[k],
             incs.at[k],
-            inc_send.at[o],
-            inc_recv.at[k],
+            inc_send.at[0],
+            inc_recv.at[0],
             {"step": lax.rem(k + o, STEPS)},
         )
 
@@ -375,8 +380,8 @@
         return remote(
             ob.at[t, h, 2 * i + side],
             att.at[t, h, c, z],
-            a2a_send.at[t, h, 2 * i + side],
-            a2a_recv.at[t, h, mine],
+            a2a_send.at[t, h],
+            a2a_recv.at[t, h],
             target,
         )
 
@@ -387,21 +392,19 @@
         other_half_came(0, 0)
         project(0, 0, both(0))
         newer(0, TILE, TILE)
-        for i in range(3):
-            far_copy(i).wait_recv()
+        came_all(far_bytes, far_recv.at[0])
         for o in (2, 1, 3):
             plane_one(o).start()
         lax.fori_loop(1, STEPS, send_inc, 0)
         onward(0, 1, 0, 2)
         onward(0, 1, 1, 2)
+        came_all(one_bytes, plane_recv.at[0])
+        for o in (2, 1, 3):
+            plane_two(o).start()
         other_half_came(0, -1)
         other_half_came(0, 1)
         project(0, 256, both(rel(-1)) + both(rel(1)))
         older(256, 768)
-        for o in (1, 3, 2):
-            plane_one(o, came=True).wait_recv()
-        for o in (2, 1, 3):
-            plane_two(o).start()
         newer(256, 768, 768)
         onward(0, 2, 0, 2)
         onward(0, 2, 1, 2)
@@ -409,15 +412,12 @@
         other_half_came(0, 2)
         project(0, 768, both(rel(-2)) + both(rel(2)))
         older(768, 1280)
-        for o in (1, 3, 2):
-            plane_two(o, came=True).wait_recv()
-        for h in range(2):
-            plane_across(c, h).start()
+        came_all(two_bytes, plane_recv.at[1])
+        plane_across(c).start()
         newer(768, 1280, 1280)
-        for h in range(2):
-            plane_across(other, h).wait_recv()
+        plane_across(other).wait_recv()
         project(0, 1280, both(3) + both(4) + both(5))
-        finish(0, 1280, (6, 5, 7, 3, 4, 1, 2, 0))
+        finish(0, 1280, (3, 4, 1, 2, 0), (6, 5, 7))
 
     def gather_second():
         other_half_came(1, 0)
@@ -425,7 +425,8 @@
         newer(0, TILE, TILE)
         onward(1, 2, 0, 4)
         for i in range(1, 5):
-            onward(1, i, 1, 4)
+            if i < 4:
+                onward(1, i, 1, 4)
             other_half_came(1, -i)
             slots = both(rel(-i))
             if i < 4:
@@ -438,8 +439,10 @@
                 older(low, high)
                 if i < 3:
                     onward(1, i + 2, 0, 4)
+                else:
+                    onward(1, 4, 1, 4)
                 newer(low, high, high)
-        finish(1, FRAMES - TILE, (7, 5, 6, 3, 4, 1, 2, 0))
+        finish(1, FRAMES - TILE, (5, 6, 3, 4, 1, 2, 0), (7,))
 
     def each_result(t, h, order, act):
         for i in order:
@@ -447,18 +450,19 @@
                 if i or side:
                     act(result_copy(t, h, i, side))
 
-    def finish(t, last, order):
-        newer(last, FRAMES, last)
-        for half in range(2):
+    def finish(t, last, old, new):
+        def settle(half, order, low):
             starts = [i * TILE + half * CHUNK for i in order]
             totals = attend(
                 jnp.concatenate([qb[r : r + CHUNK, :] for r in starts], axis=0),
-                last,
+                low,
                 FRAMES,
                 [
                     jnp.concatenate([acc[h, :, r : r + CHUNK] for r in starts], axis=1)
                     for h in range(2)
-                ],
+                ]
+                if low
+                else zeros(CHUNK * len(order)),
             )
             result = jnp.transpose(
                 jnp.concatenate([a[:64] * (1.0 / a[64:65]) for a in totals], axis=0)
@@ -473,6 +477,11 @@
                         ob[t, half, 2 * i + side] = piece
             each_result(t, half, order, lambda copy: copy.start())
 
+        settle(0, old, last)
+        settle(0, new, 0)
+        settle(1, old, last)
+        settle(1, new, 0)
+
     colour = lax.rem(x + y, 2)
 
     def owner(spot, h):
@@ -487,8 +496,8 @@
         return remote(
             sb.at[t, h, spot],
             rb.at[t, k],
-            s_send.at[t, h, spot],
-            s_recv.at[t, k],
+            s_send.at[t],
+            s_recv.at[t],
             {"step": owner(spot, h)},
         )
 
@@ -507,25 +516,13 @@
         return remote(
             nb.at[t, target],
             nr.at[t, colour, k // 2],
-            n_send.at[t, o],
-            n_recv.at[t, k],
+            n_send.at[t],
+            n_recv.at[t, colour],
             {"step": target},
         )
 
     def merge(t, h):
-        def arrive(o, carry):
-            e = lax.rem(mine + o, COLUMN)
-            zz, cc = e // 2, lax.rem(e, 2)
-            remote(
-                ob.at[t, h, 0],
-                att.at[t, h, cc, zz],
-                a2a_send.at[t, h, 0],
-                a2a_recv.at[t, h, e],
-                {"seq": zz, "cfg": cc},
-            ).wait_recv()
-            return carry
-
-        lax.fori_loop(1, COLUMN, arrive, 0)
+        came_all(ob.at[t, h, pl.ds(0, COLUMN - 1)], a2a_recv.at[t, h])
         attended = jnp.concatenate(
             [
                 jnp.concatenate([att[t, h, cc, zz] for zz in range(RING)], axis=1)
@@ -545,18 +542,7 @@
         def _():
             rb[t, k] = sb[t, h, k // 2]
 
-            def arrive(o, carry):
-                source = lax.rem(k + o, STEPS)
-                remote(
-                    sb.at[t, 0, 0],
-                    rb.at[t, source],
-                    s_send.at[t, 0, 0],
-                    s_recv.at[t, source],
-                    {"step": source},
-                ).wait_recv()
-                return carry
-
-            lax.fori_loop(1, STEPS, arrive, 0)
+            came_all(rb.at[t, pl.ds(0, STEPS - 1)], s_recv.at[t])
             terms = unfold(rb[t])
             start_rows = clip_rows()
             total = jnp.zeros_like(start_rows)
@@ -580,22 +566,14 @@
             nr[t, h, k // 2] = nb[t, k]
 
     def rows_back(t, h):
-        def arrive(j, carry):
-            source = owner(lax.rem(j + k // 2, 8), h)
-
-            @pl.when(source != k)
-            def _():
-                remote(
-                    nb.at[t, 0],
-                    nr.at[t, h, source // 2],
-                    n_send.at[t, 0],
-                    n_recv.at[t, source],
-                    {"step": source},
-                ).wait_recv()
-
-            return carry
-
-        lax.fori_loop(0, 8, arrive, 0)
+        @pl.when(colour == h)
+        def _():
+            came_all(nr.at[t, h, pl.ds(0, 7)], n_recv.at[t, h])
+
+        @pl.when(colour != h)
+        def _():
+            came_all(nr.at[t, h], n_recv.at[t, h])
+
         return unfold(nr[t, h]).reshape(HALF, WIDTH)
 
     def next_rows(h):
@@ -622,29 +600,19 @@
     def increment(j):
         return jnp.concatenate([incs[j]] * (WIDTH // 128), axis=1)
 
+    def results_left(t):
+        for h in range(2):
+            left_all(ob.at[t, h, pl.ds(0, COLUMN - 1)], a2a_send.at[t, h])
+
     def ring_left(t):
         hops = (2, 4)[t]
-        for h in range(2):
-            across(t, 0, h, c).wait_send()
-            for i in range(hops):
-                major(t, i, h).wait_send()
-                across(t, -(i + 1), h, c).wait_send()
-            for i in range(min(hops, 3)):
-                minor(t, i, h).wait_send()
-                across(t, i + 1, h, c).wait_send()
+        left_all(xall.at[t, pl.ds(0, hops), 0], maj_send.at[t])
+        left_all(xall.at[t, pl.ds(0, min(hops, 3)), 0], min_send.at[t])
+        left_all(xall.at[t, pl.ds(0, 5 if hops == 2 else RING), 0], d2d_send.at[t])
 
     def exchange_left(t):
-        def left(o, carry):
-            back_copy(t, o).wait_send()
-            return carry
-
-        lax.fori_loop(1, STEPS, left, 0)
-        for h in range(2):
-            each_owner(t, h, lambda copy: copy.wait_send())
-
-    def inc_left(o, carry):
-        inc_copy(o).wait_send()
-        return carry
+        left_all(nb.at[t, pl.ds(0, STEPS - 1)], n_send.at[t])
+        left_all(rb.at[t, pl.ds(0, STEPS - 1)], s_send.at[t])
 
     gather_first()
     loads[3].wait()
@@ -653,19 +621,7 @@
     )
     gate_copy_back.wait_recv()
 
-    def inc_arrive(o, carry):
-        source = lax.rem(k + o, STEPS)
-        remote(
-            incs.at[source],
-            incs.at[source],
-            inc_send.at[o],
-            inc_recv.at[source],
-            {"step": source},
-        ).wait_recv()
-        return carry
-
-    lax.fori_loop(1, STEPS, inc_arrive, 0)
-
+    came_all(incs.at[pl.ds(0, STEPS - 1)], inc_recv.at[0])
     merge(0, 0)
     send_terms(0, 0)
     own(0, 0)
@@ -679,16 +635,12 @@
     gate_copy.wait_send()
     ring_left(0)
     exchange_left(0)
-    for h in range(2):
-        each_result(0, h, range(8), lambda copy: copy.wait_send())
-    lax.fori_loop(1, STEPS, inc_left, 0)
-    for i in range(3):
-        far_copy(i).wait_send()
-    for h in range(2):
-        plane_across(c, h).wait_send()
-    for o in range(1, 4):
-        plane_one(o).wait_send()
-        plane_two(o).wait_send()
+    results_left(0)
+    left_all(incs.at[pl.ds(0, STEPS - 1)], inc_send.at[0])
+    left_all(far_bytes, far_send.at[0])
+    left_all(one_bytes, plane_send.at[0])
+    left_all(two_bytes, plane_send.at[1])
+    plane_across(c).wait_send()
 
     gather_second()
     ring_left(1)
@@ -696,8 +648,7 @@
     merge(1, 1)
     send_terms(1, 0)
     send_terms(1, 1)
-    for h in range(2):
-        each_result(1, h, range(8), lambda copy: copy.wait_send())
+    results_left(1)
     for h in range(2):
         own(1, h)
     own_out(0)
@@ -746,22 +697,22 @@
             pltpu.VMEM((STEPS, 8, 128), F32),
             pltpu.VMEM((2 * CHUNK, WIDTH), F32),
             dma((8,)),
-            dma((2, 4, 2)),
-            dma((2, 3, 2)),
-            dma((2, RING, 2)),
+            dma((2,)),
+            dma((2,)),
+            dma((2,)),
             dma((2, RING, 2, 2)),
-            dma((5,)),
-            dma((5,)),
-            dma((2, 4)),
-            dma((2, 4)),
-            dma((2, 2, COLUMN)),
-            dma((2, 2, COLUMN)),
-            dma((2, 2, 8)),
-            dma((2, STEPS)),
-            dma((2, STEPS)),
-            dma((2, STEPS)),
-            dma((STEPS,)),
-            dma((STEPS,)),
+            dma((2,)),
+            dma((2,)),
+            dma((2,)),
+            dma((2,)),
+            dma((2, 2)),
+            dma((2, 2)),
+            dma((2,)),
+            dma((2,)),
+            dma((2,)),
+            dma((2, 2)),
+            dma((1,)),
+            dma((1,)),
             dma((3,)),
             dma((3,)),
         ],

time: 127 us -> 121 us (0.953)
  Pallas kernels: 122 us -> 116 us
    pallas_call x1, Pallas kernels: 122 us -> 116 us  [local(): pl.pallas_call(kernel, out_shape=jax.ShapeDtypeStruct(clip.shape, F32), i...]
where the time goes in v4:
time: 121 us
  Pallas kernels  116 us (96%)
  local copies, waits for them, and re-layouts  2.31 us (2%)
  between operations  1.95 us (2%)
    pallas_call x1, Pallas kernels, local(): pl.pallas_call(kernel, out_shape=jax.ShapeDtypeStruct(clip.shape, F32), i...  116 us

profile of v4, /device:TPU:1, one launch (start us, length us, event | category | flops | bytes accessed | tf_op | source)
XLA Modules:
  0.0 120.7 jit_solution(5090509481444962769)
XLA Ops:
  1.9 116.4 %shard_map.91 = f32[256,1024]{1,0:T(8,128)} custom-call(f32[256,1024]{1,0:T(8,128)} %clip_ref.1, s32[1]{0:T(128)S(6)} %copy.11.ordinal_ref, f32[1]{0:T(128)S(6)} %copy.12.strength_ref, f32[1]{0:T(128)S(6)} %copy.13.increment_ref, bf16[50,3072]{1,0:T(8,128)(2,1)} %table_ref.1, bf16[1,3072]{1,0:T(2,128)(2,1)} %pair_ref.1, bf16[1024,3072]{1,0:T(8,128)(2,1)} %w_in_ref.1, ...), custom_call_target="tpu_custom_call" | custom-call | tf_op jit(solution)/shard_map/pallas_call | solution.py:673
  118.4 2.3 %copy.14 = f32[1,256,1024]{2,1,0:T(8,128)} copy(f32[1,256,1024]{2,1,0:T(8,128)} %bitcast.1) | data formatting | bytes 2097152

commit v5 on v4

--- a/solution.py
+++ b/solution.py
@@ -423,10 +423,8 @@
         other_half_came(1, 0)
         project(1, 0, both(0))
         newer(0, TILE, TILE)
-        onward(1, 2, 0, 4)
+        onward(1, 1, 1, 4)
         for i in range(1, 5):
-            if i < 4:
-                onward(1, i, 1, 4)
             other_half_came(1, -i)
             slots = both(rel(-i))
             if i < 4:
@@ -437,11 +435,9 @@
             project(1, low, slots)
             if i < 4:
                 older(low, high)
-                if i < 3:
-                    onward(1, i + 2, 0, 4)
-                else:
-                    onward(1, 4, 1, 4)
+                onward(1, i + 1, 0, 4)
                 newer(low, high, high)
+                onward(1, i + 1, 1, 4)
         finish(1, FRAMES - TILE, (5, 6, 3, 4, 1, 2, 0), (7,))
 
     def each_result(t, h, order, act):
@@ -594,7 +590,7 @@
         rows = pl.ds(pl.multiple_of(c * CHUNK + h * HALF, HALF), HALF)
         drift = rows_back(1, h)
         final_copy(h).start()
-        out_rows[rows, :] = clip_ref[rows, :] + drift
+        out_rows[rows, :] = drift.astype(BF16)
         out_copy(rows, h).start()
 
     def increment(j):
@@ -622,15 +618,14 @@
     gate_copy_back.wait_recv()
 
     came_all(incs.at[pl.ds(0, STEPS - 1)], inc_recv.at[0])
-    merge(0, 0)
-    send_terms(0, 0)
-    own(0, 0)
-    merge(0, 1)
-    send_terms(0, 1)
+    for h in range(2):
+        merge(0, h)
+        send_terms(0, h)
+    for h in range(2):
+        own(0, h)
     next_rows(0)
-    own(0, 1)
+    next_rows(1)
     onward(1, 1, 0, 4)
-    next_rows(1)
 
     gate_copy.wait_send()
     ring_left(0)
@@ -644,10 +639,9 @@
 
     gather_second()
     ring_left(1)
-    merge(1, 0)
-    merge(1, 1)
-    send_terms(1, 0)
-    send_terms(1, 1)
+    for h in range(2):
+        merge(1, h)
+        send_terms(1, h)
     results_left(1)
     for h in range(2):
         own(1, h)
@@ -656,7 +650,7 @@
     for h in range(2):
         rows = pl.ds(pl.multiple_of(other * CHUNK + h * HALF, HALF), HALF)
         final_copy(h).wait_recv()
-        out_rows[rows, :] = clip_ref[rows, :] + unfold(fin[h]).reshape(HALF, WIDTH)
+        out_rows[rows, :] = unfold(fin[h]).reshape(HALF, WIDTH).astype(BF16)
         out_copy(rows, 2 + h).start()
     exchange_left(1)
     for h in range(2):
@@ -672,7 +666,7 @@
     dma = pltpu.SemaphoreType.DMA
     out = pl.pallas_call(
         kernel,
-        out_shape=jax.ShapeDtypeStruct(clip.shape, F32),
+        out_shape=jax.ShapeDtypeStruct(clip.shape, BF16),
         in_specs=[vmem, smem, smem, smem, vmem, vmem, anywhere, anywhere, smem],
         out_specs=anywhere,
         scratch_shapes=[
@@ -695,7 +689,7 @@
             pltpu.VMEM((STEPS, 8, WIDTH), F32),
             pltpu.VMEM((2, 8, WIDTH), F32),
             pltpu.VMEM((STEPS, 8, 128), F32),
-            pltpu.VMEM((2 * CHUNK, WIDTH), F32),
+            pltpu.VMEM((2 * CHUNK, WIDTH), BF16),
             dma((8,)),
             dma((2,)),
             dma((2,)),
@@ -720,7 +714,7 @@
             collective_id=0, has_side_effects=True, vmem_limit_bytes=56 * 2**20
         ),
     )(clip, ordinal, strength, increment, table, pair, w_in, w_merge, sharp)
-    return out[None]
+    return (clip + out.astype(F32))[None]
 
 
 def solution(mesh):

time: 121 us -> 118 us (0.975)
  local copies, waits for them, and re-layouts: 2.31 us -> 0.01 us
  other arithmetic: 0 us -> 2.2 us
  Pallas kernels: 116 us -> 114 us
    pallas_call x1, Pallas kernels: 116 us -> 114 us  [local(): pl.pallas_call(kernel, out_shape=jax.ShapeDtypeStruct(clip.shape, BF16),...]
    unnamed x1 -> x2, local copies, waits for them, and re-layouts: 2.31 us -> 0.01 us
    broadcast_in_dim x0 -> x1, other arithmetic: none -> 2.2 us  [local(): return (clip + out.astype(F32))[None]]
where the time goes in v5:
time: 118 us
  Pallas kernels  114 us (97%)
  other arithmetic  2.2 us (2%)
  between operations  2.05 us (2%)
    pallas_call x1, Pallas kernels, local(): pl.pallas_call(kernel, out_shape=jax.ShapeDtypeStruct(clip.shape, BF16),...  114 us

profile of v5, /device:TPU:1, one launch (start us, length us, event | category | flops | bytes accessed | tf_op | source)
XLA Modules:
  0.0 118.0 jit_solution(12800063524530015510)
XLA Ops:
  0.0 0.0 copy-start
  2.0 113.8 %shard_map.91 = bf16[256,1024]{1,0:T(8,128)(2,1)} custom-call(f32[256,1024]{1,0:T(8,128)} %clip_ref.1, s32[1]{0:T(128)S(6)} %copy.10.ordinal_ref, f32[1]{0:T(128)S(6)} %copy.11.strength_ref, f32[1]{0:T(128)S(6)} %copy.12.increment_ref, bf16[50,3072]{1,0:T(8,128)(2,1)} %table_ref.1, bf16[1,3072]{1,0:T(2,128)(2,1)} %pair_ref.1, bf16[1024,3072]{1,0:T(8,128)(2,1)} %w_in_ref.1, ...), custom_call_target="tpu_custom_call" | custom-call | tf_op jit(solution)/shard_map/pallas_call | solution.py:667
  115.8 0.0 copy-done
  115.8 2.2 %add_bitcast_fusion = f32[1,256,1024]{2,1,0:T(8,128)} fusion(f32[256,1024]{1,0:T(8,128)S(1)} %copy-done, bf16[256,1024]{1,0:T(8,128)(2,1)} %shard_map.91), kind=kLoop, calls=%fused_computation | loop fusion | flops 524288 | bytes 2621440 | tf_op jit(solution)/shard_map/broadcast_in_dim | solution.py:717
Async XLA Ops:
  0.0 115.8 %copy-start = (f32[256,1024]{1,0:T(8,128)S(1)}, f32[256,1024]{1,0:T(8,128)}, u32[]{:S(2)}) copy-start(f32[256,1024]{1,0:T(8,128)} %clip_ref.1) | copy-start | bytes 3145732

commit v6 on v5

--- a/solution.py
+++ b/solution.py
@@ -134,8 +134,9 @@
     for load in loads:
         load.start()
 
-    own_rows = pl.ds(pl.multiple_of(c * CHUNK, CHUNK), CHUNK)
-    xall[0, 0, c] = layer_norm(clip_ref[own_rows, :]).astype(BF16)
+    for core in range(2):
+        rows = clip_ref[core * CHUNK : (core + 1) * CHUNK, :]
+        xall[0, 0, core] = layer_norm(rows).astype(BF16)
 
     lane = lax.broadcasted_iota(jnp.int32, (1, 128), 1)
     first_head = lane < 64
@@ -174,8 +175,6 @@
         == (lax.broadcasted_iota(jnp.int32, (128, 128), 1) < 64)
     ).astype(F32).astype(BF16)
 
-    pl.semaphore_wait(barrier, 2 * (COLUMN - 1))
-
     def left_all(block, send_sem):
         remote(block, block, send_sem, pair_recv.at[0], {"cfg": other}).wait_send()
 
@@ -225,7 +224,8 @@
     def begin(t, h):
         major(t, 0, h).start()
         minor(t, 0, h).start()
-        across(t, 0, h, c).start()
+        if t:
+            across(t, 0, h, c).start()
 
     def onward(t, i, h, hops):
         major(t, i - 1, h).wait_recv()
@@ -291,14 +291,9 @@
     one_bytes = xall.at[0, pl.ds(0, 3), 0, pl.ds(0, 32), pl.ds(0, 768)]
     two_bytes = xall.at[0, pl.ds(0, 3), 0, pl.ds(0, 96)]
 
-    for i in range(3):
-        far_copy(i).start()
-    for h in range(2):
-        begin(0, h)
     gate_copy = remote(
         gates.at[c], gates.at[c], pair_send.at[0], pair_recv.at[0], {"cfg": other}
     )
-    gate_copy.start()
 
     def inc_copy(o):
         return remote(
@@ -370,6 +365,15 @@
             for h in range(2):
                 acc[h, :, a:b] = totals[h]
 
+    project(0, 0, [(0, c), (0, other)])
+    newer(0, TILE, TILE)
+    pl.semaphore_wait(barrier, 2 * (COLUMN - 1))
+    for i in range(3):
+        far_copy(i).start()
+    for h in range(2):
+        begin(0, h)
+    gate_copy.start()
+
     def place(t, i):
         if t == 0 and i > 4:
             return i - 2
@@ -389,9 +393,6 @@
         return [(slab, c), (slab, other)]
 
     def gather_first():
-        other_half_came(0, 0)
-        project(0, 0, both(0))
-        newer(0, TILE, TILE)
         came_all(far_bytes, far_recv.at[0])
         for o in (2, 1, 3):
             plane_one(o).start()
@@ -604,7 +605,7 @@
         hops = (2, 4)[t]
         left_all(xall.at[t, pl.ds(0, hops), 0], maj_send.at[t])
         left_all(xall.at[t, pl.ds(0, min(hops, 3)), 0], min_send.at[t])
-        left_all(xall.at[t, pl.ds(0, 5 if hops == 2 else RING), 0], d2d_send.at[t])
+        left_all(xall.at[t, pl.ds(0, 4 if hops == 2 else RING), 0], d2d_send.at[t])
 
     def exchange_left(t):
         left_all(nb.at[t, pl.ds(0, STEPS - 1)], n_send.at[t])

time: 118 us -> 118 us (level)
  no operation moved by 1% of the time
where the time goes in v6:
time: 118 us
  Pallas kernels  114 us (97%)
  other arithmetic  2.2 us (2%)
  between operations  2.05 us (2%)
    pallas_call x1, Pallas kernels, local(): pl.pallas_call(kernel, out_shape=jax.ShapeDtypeStruct(clip.shape, BF16),...  114 us

profile of v6, /device:TPU:1, one launch (start us, length us, event | category | flops | bytes accessed | tf_op | source)
XLA Modules:
  0.0 118.0 jit_solution(9238013564592254074)
XLA Ops:
  0.0 0.0 copy-start
  2.0 113.7 %shard_map.91 = bf16[256,1024]{1,0:T(8,128)(2,1)} custom-call(f32[256,1024]{1,0:T(8,128)} %clip_ref.1, s32[1]{0:T(128)S(6)} %copy.10.ordinal_ref, f32[1]{0:T(128)S(6)} %copy.11.strength_ref, f32[1]{0:T(128)S(6)} %copy.12.increment_ref, bf16[50,3072]{1,0:T(8,128)(2,1)} %table_ref.1, bf16[1,3072]{1,0:T(2,128)(2,1)} %pair_ref.1, bf16[1024,3072]{1,0:T(8,128)(2,1)} %w_in_ref.1, ...), custom_call_target="tpu_custom_call" | custom-call | tf_op jit(solution)/shard_map/pallas_call | solution.py:668
  115.7 0.0 copy-done
  115.8 2.2 %add_bitcast_fusion = f32[1,256,1024]{2,1,0:T(8,128)} fusion(f32[256,1024]{1,0:T(8,128)S(1)} %copy-done, bf16[256,1024]{1,0:T(8,128)(2,1)} %shard_map.91), kind=kLoop, calls=%fused_computation | loop fusion | flops 524288 | bytes 2621440 | tf_op jit(solution)/shard_map/broadcast_in_dim | solution.py:718
Async XLA Ops:
  0.0 115.7 %copy-start = (f32[256,1024]{1,0:T(8,128)S(1)}, f32[256,1024]{1,0:T(8,128)}, u32[]{:S(2)}) copy-start(f32[256,1024]{1,0:T(8,128)} %clip_ref.1) | copy-start | bytes 3145732
